TPU v7x, 512 devices: a whole 4x8x8 slice. The times are simulated.
512 devices in a mesh: mat: 4 (over z_hi), row: 64 (over y, x, core), col: 2 (over z_lo).
Axes of the slice: x: 4, y: 8, z: 8 (z_hi: 4, z_lo: 2; z = z_hi * 2 + z_lo), core: 2. Of those that a mesh axis runs over, the one named last changes fastest.
Arguments:
- iterate: float32 [10752, 10752], P(('mat', 'row'), 'col'), parts along dimension 0, may hold values from -1 to 1, as said below
Outputs:
- update: float32 [10752, 10752], P(('mat', 'row'), 'col'), parts along dimension 0
There are 4 independent parts, one for each index of `mat`. A program takes and returns all parts, laid end to end along the dimension named above; each array names one. Nothing has to cross between parts.
Inputs may be any that keep to these rules, and one draw needn't show every extreme that they name: An iterate of earlier Newton-Schulz steps: a full-rank matrix whose largest singular value is below 2.
All inputs are finite; a program needn't handle non-finite values.
Results may differ from a plain program's by a relative error of at most 0.015.
Values may be sent and summed in bfloat16 or wider, within the bound.
A program may use at most 64 MiB of HBM per device.

v0:
```python
import math

import jax
import jax.numpy as jnp
from jax import lax
from jax.sharding import PartitionSpec as P

COLS = 10752


linear_term = 3.4445
cubic_term = -4.775
quintic_term = 2.0315


def partner_2(value, axis, bit):
    mask = 2**bit
    pairs = [(source, source ^ mask) for source in range(lax.axis_size(axis))]
    return lax.ppermute(value, axis, pairs)


def product(former, latter):
    return jnp.dot(former, latter, preferred_element_type=jnp.float32)


def ordered(current, arrived, leading, concat_dim):
    return jnp.concatenate(
        [jnp.where(leading, current, arrived), jnp.where(leading, arrived, current)],
        axis=concat_dim,
    )


def permute_blocks(matrix, axis_number, own_place, group_size):
    if axis_number == 1:
        return permute_blocks(matrix.T, 0, own_place, group_size).T
    block_rows = matrix.shape[0] // group_size
    places = jnp.bitwise_xor(jnp.arange(group_size, dtype=jnp.int32), own_place)
    blocks = matrix.reshape(group_size, block_rows, matrix.shape[1])
    return jnp.take(blocks, places, axis=0).reshape(matrix.shape)


def on_device(iterate):
    row_index = lax.axis_index("row")
    group_bits = (lax.axis_size("row").bit_length() - 1) // 2
    group_size = 1 << group_bits
    near_bits = list(range(group_bits))
    far_bits = list(range(group_bits, 2 * group_bits))
    near_place = row_index % group_size
    far_place = row_index // group_size % group_size

    def own_bit(bit_number):
        return row_index // (1 << bit_number) % 2 == 0

    rounded = iterate.astype(jnp.bfloat16)
    block_run = rounded
    for bit_number in near_bits:
        arrived = partner_2(block_run, "row", bit_number)
        block_run = jnp.concatenate([block_run, arrived], axis=0)
    strided = rounded
    for bit_number in far_bits:
        arrived = partner_2(strided, "row", bit_number)
        strided = jnp.concatenate([strided, arrived], axis=0)
    partial_value = lax.dot_general(
        block_run, strided, (((1,), (1,)), ((), ())), preferred_element_type=jnp.float32
    )
    gram_tile = lax.psum(partial_value, "col").astype(jnp.bfloat16)
    gram_tile = permute_blocks(
        permute_blocks(gram_tile, 0, near_place, group_size), 1, far_place, group_size
    )
    row_tiles = gram_tile
    for bit_number in near_bits:
        arrived = partner_2(row_tiles, "row", bit_number)
        row_tiles = ordered(row_tiles, arrived, own_bit(bit_number), 1)
    super_rows = gram_tile.shape[0]
    row_tiles = (
        row_tiles.reshape(super_rows, group_size, group_size, -1)
        .transpose(0, 2, 1, 3)
        .reshape(super_rows, -1)
    )
    column_tiles = gram_tile
    for bit_number in far_bits:
        arrived = partner_2(column_tiles, "row", bit_number)
        column_tiles = ordered(column_tiles, arrived, own_bit(bit_number), 0)
    square = product(row_tiles, column_tiles)
    polynomial = (cubic_term * gram_tile.astype(jnp.float32) + quintic_term * square).astype(
        jnp.bfloat16
    )

    def exchange_far(outgoing, bit_number):
        return partner_2(outgoing, "row", bit_number)

    weights = permute_blocks(polynomial, 0, near_place, group_size).T
    bit_list = far_bits[::-1]
    half_rows = weights.shape[0] // 2
    keep_low = own_bit(bit_list[0])
    retained = product(jnp.where(keep_low, weights[:half_rows], weights[half_rows:]), block_run)
    outgoing = product(jnp.where(keep_low, weights[half_rows:], weights[:half_rows]), block_run)
    summed = retained + exchange_far(outgoing, bit_list[0])
    for bit_number in bit_list[1:]:
        half_rows = summed.shape[0] // 2
        keep_low = own_bit(bit_number)
        retained = jnp.where(keep_low, summed[:half_rows], summed[half_rows:])
        outgoing = jnp.where(keep_low, summed[half_rows:], summed[:half_rows])
        summed = retained + exchange_far(outgoing, bit_number)
    return math.sqrt(COLS) * (linear_term * rounded.astype(jnp.float32) + summed)


def solution(mesh):
    in_specs = (P(("mat", "row"), "col"),)
    out_specs = P(("mat", "row"), "col")
    return jax.shard_map(
        on_device, mesh=mesh, in_specs=in_specs, out_specs=out_specs, check_vma=False
    )
```

profile of v0, /device:TPU:1, one launch (start us, length us, event | category | flops | bytes accessed | tf_op | source)
XLA Modules:
  0.0 547.9 jit_solution(5081067488304750981)
XLA Ops:
  1.3 4.0 collective-permute-start.3
  5.3 6.7 %collective-permute-start = (bf16[42,5376]{1,0:T(8,128)(2,1)S(1)}, bf16[42,5376]{1,0:T(8,128)(2,1)S(1)}, u32[]{:S(2)}, u32[]{:S(2)}) collective-permute-start(bf16[42,5376]{1,0:T(8,128)(2,1)S(1)} %convert_element_type.15), channel_id=1, source_target_pairs={{0,2},{2,0},{4,6},{6,4},{8,10},{10,8},{12,14},{14,12},{16,18},{18,... | collective-permute-start | bytes 1354760 | tf_op jit(solution)/shard_map/ppermute | solution.py:19
  13.8 6.2 %collective-permute-start.1 = (bf16[84,5376]{1,0:T(8,128)(2,1)S(1)}, bf16[84,5376]{1,0:T(8,128)(2,1)S(1)}, u32[]{:S(2)}, u32[]{:S(2)}) collective-permute-start(bf16[84,5376]{1,0:T(8,128)(2,1)S(1)} %get-tuple-element.20), channel_id=1, source_target_pairs={{0,4},{2,6},{4,0},{6,2},{8,12},{10,14},{12,8},{14,10},{16,20},{18,... | collective-permute-start | bytes 2709512 | tf_op jit(solution)/shard_map/ppermute | solution.py:19
  20.0 4.2 collective-permute-start.4
  24.3 14.5 %collective-permute-done.1 = bf16[84,5376]{1,0:T(8,128)(2,1)S(1)} collective-permute-done((bf16[84,5376]{1,0:T(8,128)(2,1)S(1)}, bf16[84,5376]{1,0:T(8,128)(2,1)S(1)}, u32[]{:S(2)}, u32[]{:S(2)}) %collective-permute-start.1) | collective-permute-done | bytes 903200 | tf_op jit(solution)/shard_map/ppermute | solution.py:19
  38.7 26.2 %collective-permute-done.4 = bf16[84,5376]{1,0:T(8,128)(2,1)S(1)} collective-permute-done((bf16[84,5376]{1,0:T(8,128)(2,1)S(1)}, bf16[84,5376]{1,0:T(8,128)(2,1)S(1)}, u32[]{:S(2)}, u32[]{:S(2)}) %collective-permute-start.4) | collective-permute-done | bytes 903200 | tf_op jit(solution)/shard_map/ppermute | solution.py:19
  66.8 4.3 collective-permute-start.2
  71.2 8.4 %collective-permute-start.5 = (bf16[168,5376]{1,0:T(8,128)(2,1)S(1)}, bf16[168,5376]{1,0:T(8,128)(2,1)}, u32[]{:S(2)}, u32[]{:S(2)}) collective-permute-start(bf16[168,5376]{1,0:T(8,128)(2,1)S(1)} %get-tuple-element.19), channel_id=1, source_target_pairs={{0,64},{2,66},{4,68},{6,70},{8,72},{10,74},{12,76},{14,78},{16,80}... | collective-permute-start | bytes 5419016 | tf_op jit(solution)/shard_map/ppermute | solution.py:19
  79.7 30.1 %collective-permute-done.2 = bf16[168,5376]{1,0:T(8,128)(2,1)} collective-permute-done((bf16[168,5376]{1,0:T(8,128)(2,1)}, bf16[168,5376]{1,0:T(8,128)(2,1)}, u32[]{:S(2)}, u32[]{:S(2)}) %collective-permute-start.2) | collective-permute-done | bytes 1806368 | tf_op jit(solution)/shard_map/ppermute | solution.py:19
  109.8 47.8 %collective-permute-done.5 = bf16[168,5376]{1,0:T(8,128)(2,1)} collective-permute-done((bf16[168,5376]{1,0:T(8,128)(2,1)S(1)}, bf16[168,5376]{1,0:T(8,128)(2,1)}, u32[]{:S(2)}, u32[]{:S(2)}) %collective-permute-start.5) | collective-permute-done | bytes 1806368 | tf_op jit(solution)/shard_map/ppermute | solution.py:19
  157.7 4.6 fusion.4
  162.3 14.0 %all-reduce.1 = bf16[336,336]{1,0:T(8,128)(2,1)S(1)} all-reduce(f32[336,336]{1,0:T(8,128)S(1)} %fusion.4), channel_id=1, replica_groups=mesh['mat'=4,'row'=64,'col'=2] {'col'}, use_global_device_ids=true, to_apply=%region_0.1 | all-reduce | flops 112896 | bytes 677376 | tf_op jit(solution)/shard_map/psum | solution.py:66
  178.6 5.9 %collective-permute-start.6 = (bf16[336,336]{1,0:T(8,128)(2,1)S(1)}, bf16[336,336]{1,0:T(8,128)(2,1)S(1)}, u32[]{:S(2)}, u32[]{:S(2)}) collective-permute-start(bf16[336,336]{1,0:T(8,128)(2,1)S(1)} %bitcast.15), channel_id=1, source_target_pairs={{0,2},{2,0},{4,6},{6,4},{8,10},{10,8},{12,14},{14,12},{16,18},{18,... | collective-permute-start | bytes 677384 | tf_op jit(solution)/shard_map/ppermute | solution.py:19
  186.5 7.8 %collective-permute-done.9 = bf16[336,336]{1,0:T(8,128)(2,1)S(1)} collective-permute-done((bf16[336,336]{1,0:T(8,128)(2,1)S(1)}, bf16[336,336]{1,0:T(8,128)(2,1)S(1)}, u32[]{:S(2)}, u32[]{:S(2)}) %collective-permute-start.9) | collective-permute-done | bytes 225824 | tf_op jit(solution)/shard_map/ppermute | solution.py:19
  196.6 4.3 collective-permute-start.10
  200.9 8.0 %collective-permute-done.7 = bf16[336,672]{1,0:T(8,128)(2,1)S(1)} collective-permute-done((bf16[336,672]{1,0:T(8,128)(2,1)S(1)}, bf16[336,672]{1,0:T(8,128)(2,1)S(1)}, u32[]{:S(2)}, u32[]{:S(2)}) %collective-permute-start.7) | collective-permute-done | bytes 451616 | tf_op jit(solution)/shard_map/ppermute | solution.py:19
  212.9 10.3 %collective-permute-done.10 = bf16[672,336]{1,0:T(8,128)(2,1)} collective-permute-done((bf16[672,336]{1,0:T(8,128)(2,1)S(1)}, bf16[672,336]{1,0:T(8,128)(2,1)}, u32[]{:S(2)}, u32[]{:S(2)}) %collective-permute-start.10) | collective-permute-done | bytes 451616 | tf_op jit(solution)/shard_map/ppermute | solution.py:19
  226.5 4.6 collective-permute-start.11
  243.8 4.2 reshape.34
  248.0 27.5 %collective-permute-done.11 = bf16[1344,336]{0,1:T(8,128)(2,1)} collective-permute-done((bf16[1344,336]{0,1:T(8,128)(2,1)}, bf16[1344,336]{0,1:T(8,128)(2,1)}, u32[]{:S(2)}, u32[]{:S(2)}) %collective-permute-start.11) | collective-permute-done | bytes 903200 | tf_op jit(solution)/shard_map/ppermute | solution.py:19
  284.1 4.7 collective-permute-start.12
  288.8 143.6 %collective-permute-done.12 = f32[168,5376]{1,0:T(8,128)S(1)} collective-permute-done((f32[168,5376]{1,0:T(8,128)S(1)}, f32[168,5376]{1,0:T(8,128)S(1)}, u32[]{:S(2)}, u32[]{:S(2)}) %collective-permute-start.12) | collective-permute-done | bytes 3612704 | tf_op jit(solution)/shard_map/ppermute | solution.py:19
  437.5 83.7 %collective-permute-done.13 = f32[84,5376]{1,0:T(8,128)S(1)} collective-permute-done((f32[84,5376]{1,0:T(8,128)S(1)}, f32[84,5376]{1,0:T(8,128)S(1)}, u32[]{:S(2)}, u32[]{:S(2)}) %collective-permute-start.13) | collective-permute-done | bytes 1806368 | tf_op jit(solution)/shard_map/ppermute | solution.py:19
  523.7 22.9 %collective-permute-done.14 = f32[42,5376]{1,0:T(8,128)S(1)} collective-permute-done((f32[42,5376]{1,0:T(8,128)S(1)}, f32[42,5376]{1,0:T(8,128)S(1)}, u32[]{:S(2)}, u32[]{:S(2)}) %collective-permute-start.14) | collective-permute-done | bytes 903200 | tf_op jit(solution)/shard_map/ppermute | solution.py:19
  (76 shorter events, 48.4 us)
Async XLA Ops:
  1.3 156.4 %copy-start = (bf16[42,5376]{1,0:T(8,128)(2,1)}, bf16[42,5376]{1,0:T(8,128)(2,1)S(1)}, u32[]{:S(2)}) copy-start(bf16[42,5376]{1,0:T(8,128)(2,1)S(1)} %convert_element_type.15) | copy-start | bytes 1354756
  1.3 10.7 %collective-permute-start.3 = (bf16[42,5376]{1,0:T(8,128)(2,1)S(1)}, bf16[42,5376]{1,0:T(8,128)(2,1)S(1)}, u32[]{:S(2)}, u32[]{:S(2)}) collective-permute-start(bf16[42,5376]{1,0:T(8,128)(2,1)S(1)} %convert_element_type.15), channel_id=1, source_target_pairs={{0,16},{2,18},{4,20},{6,22},{8,24},{10,26},{12,28},{14,30},{16,0},... | collective-permute-start | bytes 1354760 | tf_op jit(solution)/shard_map/ppermute | solution.py:19
  5.3 8.2 %collective-permute-start = (bf16[42,5376]{1,0:T(8,128)(2,1)S(1)}, bf16[42,5376]{1,0:T(8,128)(2,1)S(1)}, u32[]{:S(2)}, u32[]{:S(2)}) collective-permute-start(bf16[42,5376]{1,0:T(8,128)(2,1)S(1)} %convert_element_type.15), channel_id=1, source_target_pairs={{0,2},{2,0},{4,6},{6,4},{8,10},{10,8},{12,14},{14,12},{16,18},{18,... | collective-permute-start | bytes 1354760 | tf_op jit(solution)/shard_map/ppermute | solution.py:19
  13.5 144.2 %copy-start.4 = (bf16[42,5376]{1,0:T(8,128)(2,1)}, bf16[42,5376]{1,0:T(8,128)(2,1)S(1)}, u32[]{:S(2)}) copy-start(bf16[42,5376]{1,0:T(8,128)(2,1)S(1)} %collective-permute-done) | copy-start | bytes 1354756
  13.8 24.9 %collective-permute-start.1 = (bf16[84,5376]{1,0:T(8,128)(2,1)S(1)}, bf16[84,5376]{1,0:T(8,128)(2,1)S(1)}, u32[]{:S(2)}, u32[]{:S(2)}) collective-permute-start(bf16[84,5376]{1,0:T(8,128)(2,1)S(1)} %get-tuple-element.20), channel_id=1, source_target_pairs={{0,4},{2,6},{4,0},{6,2},{8,12},{10,14},{12,8},{14,10},{16,20},{18,... | collective-permute-start | bytes 2709512 | tf_op jit(solution)/shard_map/ppermute | solution.py:19
  20.0 44.9 %collective-permute-start.4 = (bf16[84,5376]{1,0:T(8,128)(2,1)S(1)}, bf16[84,5376]{1,0:T(8,128)(2,1)S(1)}, u32[]{:S(2)}, u32[]{:S(2)}) collective-permute-start(bf16[84,5376]{1,0:T(8,128)(2,1)S(1)} %get-tuple-element.21), channel_id=1, source_target_pairs={{0,32},{2,34},{4,36},{6,38},{8,40},{10,42},{12,44},{14,46},{16,48}... | collective-permute-start | bytes 2709512 | tf_op jit(solution)/shard_map/ppermute | solution.py:19
  38.7 40.9 %copy-start.8 = (bf16[84,5376]{1,0:T(8,128)(2,1)}, bf16[84,5376]{1,0:T(8,128)(2,1)S(1)}, u32[]{:S(2)}) copy-start(bf16[84,5376]{1,0:T(8,128)(2,1)S(1)} %collective-permute-done.1) | copy-start | bytes 2709508
  64.9 14.7 %copy-start.10 = (bf16[84,5376]{1,0:T(8,128)(2,1)}, bf16[84,5376]{1,0:T(8,128)(2,1)S(1)}, u32[]{:S(2)}) copy-start(bf16[84,5376]{1,0:T(8,128)(2,1)S(1)} %collective-permute-done.4) | copy-start | bytes 2709508
  66.8 43.0 %collective-permute-start.2 = (bf16[168,5376]{1,0:T(8,128)(2,1)}, bf16[168,5376]{1,0:T(8,128)(2,1)}, u32[]{:S(2)}, u32[]{:S(2)}) collective-permute-start(bf16[168,5376]{1,0:T(8,128)(2,1)} %get-tuple-element.18), channel_id=1, source_target_pairs={{0,8},{2,10},{4,12},{6,14},{8,0},{10,2},{12,4},{14,6},{16,24},{18,... | collective-permute-start | bytes 5419016 | tf_op jit(solution)/shard_map/ppermute | solution.py:19
  71.2 86.5 %collective-permute-start.5 = (bf16[168,5376]{1,0:T(8,128)(2,1)S(1)}, bf16[168,5376]{1,0:T(8,128)(2,1)}, u32[]{:S(2)}, u32[]{:S(2)}) collective-permute-start(bf16[168,5376]{1,0:T(8,128)(2,1)S(1)} %get-tuple-element.19), channel_id=1, source_target_pairs={{0,64},{2,66},{4,68},{6,70},{8,72},{10,74},{12,76},{14,78},{16,80}... | collective-permute-start | bytes 5419016 | tf_op jit(solution)/shard_map/ppermute | solution.py:19
  178.6 22.3 %copy-start.6 = (bf16[336,336]{0,1:T(8,128)(2,1)}, bf16[336,336]{0,1:T(8,128)(2,1)S(1)}, u32[]{:S(2)}) copy-start(bf16[336,336]{0,1:T(8,128)(2,1)S(1)} %copy.7) | copy-start | bytes 677380
  178.6 7.9 %collective-permute-start.6 = (bf16[336,336]{1,0:T(8,128)(2,1)S(1)}, bf16[336,336]{1,0:T(8,128)(2,1)S(1)}, u32[]{:S(2)}, u32[]{:S(2)}) collective-permute-start(bf16[336,336]{1,0:T(8,128)(2,1)S(1)} %bitcast.15), channel_id=1, source_target_pairs={{0,2},{2,0},{4,6},{6,4},{8,10},{10,8},{12,14},{14,12},{16,18},{18,... | collective-permute-start | bytes 677384 | tf_op jit(solution)/shard_map/ppermute | solution.py:19
  184.5 9.7 %collective-permute-start.9 = (bf16[336,336]{1,0:T(8,128)(2,1)S(1)}, bf16[336,336]{1,0:T(8,128)(2,1)S(1)}, u32[]{:S(2)}, u32[]{:S(2)}) collective-permute-start(bf16[336,336]{1,0:T(8,128)(2,1)S(1)} %bitcast.16), channel_id=1, source_target_pairs={{0,16},{2,18},{4,20},{6,22},{8,24},{10,26},{12,28},{14,30},{16,0},... | collective-permute-start | bytes 677384 | tf_op jit(solution)/shard_map/ppermute | solution.py:19
  194.5 14.4 %collective-permute-start.7 = (bf16[336,672]{1,0:T(8,128)(2,1)S(1)}, bf16[336,672]{1,0:T(8,128)(2,1)S(1)}, u32[]{:S(2)}, u32[]{:S(2)}) collective-permute-start(bf16[336,672]{1,0:T(8,128)(2,1)S(1)} %pad_maximum_fusion.9), channel_id=1, source_target_pairs={{0,4},{2,6},{4,0},{6,2},{8,12},{10,14},{12,8},{14,10},{16,20},{18,... | collective-permute-start | bytes 1354760 | tf_op jit(solution)/shard_map/ppermute | solution.py:19
  196.6 26.7 %collective-permute-start.10 = (bf16[672,336]{1,0:T(8,128)(2,1)S(1)}, bf16[672,336]{1,0:T(8,128)(2,1)}, u32[]{:S(2)}, u32[]{:S(2)}) collective-permute-start(bf16[672,336]{1,0:T(8,128)(2,1)S(1)} %pad_maximum_fusion.10), channel_id=1, source_target_pairs={{0,32},{2,34},{4,36},{6,38},{8,40},{10,42},{12,44},{14,46},{16,48}... | collective-permute-start | bytes 1354760 | tf_op jit(solution)/shard_map/ppermute | solution.py:19
  210.4 24.5 %collective-permute-start.8 = (bf16[336,1344]{1,0:T(8,128)(2,1)}, bf16[336,1344]{1,0:T(8,128)(2,1)}, u32[]{:S(2)}, u32[]{:S(2)}) collective-permute-start(bf16[336,1344]{1,0:T(8,128)(2,1)} %pad_maximum_fusion.8), channel_id=1, source_target_pairs={{0,8},{2,10},{4,12},{6,14},{8,0},{10,2},{12,4},{14,6},{16,24},{18,... | collective-permute-start | bytes 2709512 | tf_op jit(solution)/shard_map/ppermute | solution.py:19
  226.5 49.0 %collective-permute-start.11 = (bf16[1344,336]{0,1:T(8,128)(2,1)}, bf16[1344,336]{0,1:T(8,128)(2,1)}, u32[]{:S(2)}, u32[]{:S(2)}) collective-permute-start(bf16[1344,336]{0,1:T(8,128)(2,1)} %copy.10), channel_id=1, source_target_pairs={{0,64},{2,66},{4,68},{6,70},{8,72},{10,74},{12,76},{14,78},{16,80}... | collective-permute-start | bytes 2709512 | tf_op jit(solution)/shard_map/ppermute | solution.py:19
  248.0 30.0 %copy-start.7 = (bf16[336,336]{0,1:T(8,128)(2,1)S(1)}, bf16[336,336]{0,1:T(8,128)(2,1)}, u32[]{:S(2)}) copy-start(bf16[336,336]{0,1:T(8,128)(2,1)} %copy-done.6) | copy-start | bytes 677380
  279.1 2.1 copy-start.5
  279.1 2.1 copy-start.9
  284.1 148.3 %collective-permute-start.12 = (f32[168,5376]{1,0:T(8,128)S(1)}, f32[168,5376]{1,0:T(8,128)S(1)}, u32[]{:S(2)}, u32[]{:S(2)}) collective-permute-start(f32[168,5376]{1,0:T(8,128)S(1)} %fusion.24), channel_id=1, source_target_pairs={{0,64},{2,66},{4,68},{6,70},{8,72},{10,74},{12,76},{14,78},{16,80}... | collective-permute-start | bytes 10838024 | tf_op jit(solution)/shard_map/ppermute | solution.py:19
  435.4 111.2 %copy-start.2 = (f32[42,5376]{1,0:T(8,128)S(1)}, f32[42,5376]{1,0:T(8,128)}, u32[]{:S(2)}) copy-start(f32[42,5376]{1,0:T(8,128)} %param.3) | copy-start | bytes 2709508
  435.4 85.8 %collective-permute-start.13 = (f32[84,5376]{1,0:T(8,128)S(1)}, f32[84,5376]{1,0:T(8,128)S(1)}, u32[]{:S(2)}, u32[]{:S(2)}) collective-permute-start(f32[84,5376]{1,0:T(8,128)S(1)} %slice_select_fusion), channel_id=1, source_target_pairs={{0,32},{2,34},{4,36},{6,38},{8,40},{10,42},{12,44},{14,46},{16,48}... | collective-permute-start | bytes 5419016 | tf_op jit(solution)/shard_map/ppermute | solution.py:19
  521.7 24.9 %collective-permute-start.14 = (f32[42,5376]{1,0:T(8,128)S(1)}, f32[42,5376]{1,0:T(8,128)S(1)}, u32[]{:S(2)}, u32[]{:S(2)}) collective-permute-start(f32[42,5376]{1,0:T(8,128)S(1)} %slice_select_fusion.1), channel_id=1, source_target_pairs={{0,16},{2,18},{4,20},{6,22},{8,24},{10,26},{12,28},{14,30},{16,0},... | collective-permute-start | bytes 2709512 | tf_op jit(solution)/shard_map/ppermute | solution.py:19
  (2 other events, 3.7 us)
where the time goes:
time: 550 us; the launch traced here: 548 us
  waiting for transfers between devices  428 us (78%)
  starting transfers between devices  63.8 us (12%)
  local copies, waits for them, and re-layouts  18.8 us (3%)
  blocking collectives  14 us (3%)
  other arithmetic  11.6 us (2%)
  matrix products  11.4 us (2%)
    ppermute x15, waiting for transfers between devices, partner_2(): return lax.ppermute(value, axis, pairs)  428 us
    ppermute x15, starting transfers between devices, partner_2(): return lax.ppermute(value, axis, pairs)  63.8 us
    psum x1, blocking collectives, on_device(): gram_tile = lax.psum(partial_value, 'col').astype(jnp.bfloat16)  14 us
  transfers between devices with their start and end apart: 15, of which 13 were waited for; matrix products, arithmetic and copies ran while one was open for 3% of the time, Pallas kernels for 0%

commit v1 on v0

v1 whole, which is shorter than its diff:
```python
import functools
import math

import jax
import jax.numpy as jnp
from jax import lax
from jax.experimental import pallas as pl
from jax.experimental.pallas import tpu as pltpu
from jax.sharding import PartitionSpec as P

COLS = 10752

linear_term = 3.4445
cubic_term = -4.775
quintic_term = 2.0315

NY = 8
NX = 4
NP = 8
OWN = 42
PAD = 48
DENSE = NY * OWN
TALL = NY * PAD
FULL = NP * DENSE
WIDE = 768
SPLIT = 384
PARTS = ((0, SPLIT), (SPLIT, WIDE - SPLIT))
HALVES = ((0, 1408), (1408, 1280))


def dot(a, b, dims=((1,), (0,))):
    return lax.dot_general(a, b, (dims, ((), ())), preferred_element_type=jnp.float32)


def kernel(x_ref, y_ref, xs, sel, a2a, xg, wg, gp, rb, zs, zr, gf, yp,
           in_s, in_r, ag_s, ag_r, rs_s, rs_r, z_s, z_r, gg_s, gg_r, out_s, out_r):
    m, r, z = lax.axis_index("mat"), lax.axis_index("row"), lax.axis_index("col")
    y, p = r // NP, r % NP
    x, c = p // 2, p % 2
    pending = []

    def dev(yy, xx, cc):
        return (m, (yy % NY) * NP + (xx % NX) * 2 + cc, z)

    def copy(src, dst, ssem, rsem, to):
        return pltpu.make_async_remote_copy(
            src_ref=src, dst_ref=dst, send_sem=ssem, recv_sem=rsem,
            device_id=to, device_id_type=pl.DeviceIdType.MESH)

    def send(src, dst, ssem, rsem, to):
        op = copy(src, dst, ssem, rsem, to)
        op.start()
        pending.append(op)

    def arrive(dst, ssem, rsem, to):
        copy(dst, dst, ssem, rsem, to).wait_recv()

    sibling = dev(y, x, 1 - c)
    east, west = dev(y, x + 1, c), dev(y, x + 3, c)
    other_z = (m, r, 1 - z)
    ydev = [dev(y + k, x, c) for k in range(NY)]

    a2a[:, 640:768] = jnp.zeros((TALL, 128), jnp.bfloat16)
    barrier = pltpu.get_barrier_semaphore()
    for to in ydev[1:] + [sibling, east, west, other_z]:
        pl.semaphore_signal(barrier, inc=1, device_id=to, device_id_type=pl.DeviceIdType.MESH)

    xs[32:48, :] = jnp.zeros((16, xs.shape[1]), jnp.bfloat16)
    xs[0:OWN, :] = x_ref[...].astype(jnp.bfloat16)
    row = lax.broadcasted_iota(jnp.int32, (DENSE, TALL), 0)
    col = lax.broadcasted_iota(jnp.int32, (DENSE, TALL), 1)
    place = row
    for k in range(1, NY):
        place = place + jnp.where(row >= OWN * k, PAD - OWN, 0)
    sel[...] = jnp.where(col == place, 1.0, 0.0).astype(jnp.bfloat16)
    pl.semaphore_wait(barrier, NY + 3)

    def first(yy):
        return pl.multiple_of((21 * yy) // 4 * 128, 128)

    def block(yy):
        return pl.ds(pl.multiple_of((yy % NY) * PAD, 16), PAD)

    def rows(xx, cc):
        return pl.ds(pl.multiple_of(((xx % NX) * 2 + cc) * DENSE, 16), DENSE)

    cuts = ((0, 384), (384, 256), (640, 128))
    order = (4, 3, 5, 2, 6, 1, 7)

    for i, (off, size) in enumerate(cuts):
        for k in order:
            t = (y + k) % NY

            def go(k=k, t=t, i=i, off=off, size=size, start=True):
                op = copy(xs.at[:, pl.ds(pl.multiple_of(first(t) + off, 128), size)],
                          a2a.at[block(y), off:off + size],
                          in_s.at[i, k - 1], in_r.at[i, k - 1], ydev[k])
                if start:
                    op.start()
                else:
                    op.wait_send()
            if i < 2:
                go()
            else:
                pl.when(t % 4 == 3)(go)

    for i, (off, size) in enumerate(cuts):
        def own(off=off, size=size):
            a2a[block(y), off:off + size] = xs[:, pl.ds(pl.multiple_of(first(y) + off, 128), size)]
        if i < 2:
            own()
        else:
            pl.when(y % 4 == 3)(own)

    def in_wait(i):
        off, size = cuts[i]
        for k in order:
            arrive(a2a.at[block(y - k + NY), off:off + size],
                   in_s.at[i, k - 1], in_r.at[i, k - 1], ydev[k])

    def lanes(ch):
        return slice(PARTS[ch][0], PARTS[ch][0] + PARTS[ch][1])

    def gather_start(buf, ch, n):
        mine = buf.at[rows(x, c), lanes(ch)]
        for q, to in enumerate((east, west, sibling)):
            send(mine, mine, ag_s.at[n, ch, q], ag_r.at[n, ch, q], to)

    def gather_end(buf, ch, n):
        def part(xx, cc):
            return buf.at[rows(xx, cc), lanes(ch)]

        def wait(ref, q):
            arrive(ref, ag_s.at[n, ch, q], ag_r.at[n, ch, q], sibling)

        def forward(ref, q, to):
            send(ref, ref, ag_s.at[n, ch, q], ag_r.at[n, ch, q], to)
        wait(part(x + 3, c), 0)
        if ch == 0:
            forward(part(x + 3, c), 3, east)
        forward(part(x + 3, c), 4, sibling)
        wait(part(x + 1, c), 1)
        if ch == 1:
            forward(part(x + 1, c), 3, west)
        forward(part(x + 1, c), 5, sibling)
        wait(part(x + 2, c), 3)
        forward(part(x + 2, c), 6, sibling)
        wait(part(x, 1 - c), 2)
        wait(part(x + 3, 1 - c), 4)
        wait(part(x + 1, 1 - c), 5)
        wait(part(x + 2, 1 - c), 6)

    for ch in range(2):
        in_wait(ch)
        if ch == 1:
            pl.when(y % 4 == 3)(functools.partial(in_wait, 2))
        xg[rows(x, c), lanes(ch)] = dot(sel[...], a2a[:, lanes(ch)]).astype(jnp.bfloat16)
        gather_start(xg, ch, 0)
    for ch in range(2):
        gather_end(xg, ch, 0)

    @pl.loop(0, 7)
    def _(j):
        at = pl.ds(pl.multiple_of(j * 384, 128), 384)
        gp[:, at] = dot(a2a[...], xg[at, :], ((1,), (1,))).astype(jnp.bfloat16)

    def half(h):
        return slice(HALVES[h][0], HALVES[h][0] + HALVES[h][1])

    def f32(v):
        return v.astype(jnp.float32)

    ways = (ydev[1], ydev[NY - 1])
    signs = (1, NY - 1)
    for k in range(4):
        for d in range(2):
            for h in range(2):
                k0 = 0 if d == h else 1
                if k < k0:
                    continue
                t = block(y + signs[d] * (4 - k))
                if k > k0:
                    arrive(rb.at[d, k - 1, :, half(h)], rs_s.at[d, k - 1, h], rs_r.at[d, k - 1, h], ways[d])
                    gp[t, half(h)] = (f32(gp[t, half(h)]) + f32(rb[d, k - 1, :, half(h)])).astype(jnp.bfloat16)
                send(gp.at[t, half(h)], rb.at[d, k, :, half(h)], rs_s.at[d, k, h], rs_r.at[d, k, h], ways[d])
    for h in range(2):
        for d in range(2):
            arrive(rb.at[d, 3, :, half(h)], rs_s.at[d, 3, h], rs_r.at[d, 3, h], ways[d])
        total = f32(gp[block(y), half(h)]) + f32(rb[0, 3, :, half(h)]) + f32(rb[1, 3, :, half(h)])
        zs[:, half(h)] = total.astype(jnp.bfloat16)
        send(zs.at[:, half(h)], zr.at[:, half(h)], z_s.at[h], z_r.at[h], other_z)
    for k in range(4):
        for h in range(2):
            if k == 0:
                arrive(zr.at[:, half(h)], z_s.at[h], z_r.at[h], other_z)
                gf[block(y), half(h)] = (f32(zs[:, half(h)]) + f32(zr[:, half(h)])).astype(jnp.bfloat16)
            for d in range(2):
                ref = gf.at[block(y + (NY - signs[d]) * k), half(h)]
                if k > 0:
                    arrive(ref, gg_s.at[d, k - 1, h], gg_r.at[d, k - 1, h], ways[d])
                if k < 3 or d == h:
                    send(ref, ref, gg_s.at[d, k, h], gg_r.at[d, k, h], ways[d])
    for d in range(2):
        arrive(gf.at[block(y + 4), half(d)], gg_s.at[d, 3, d], gg_r.at[d, 3, d], ways[d])

    for ch in range(2):
        inner = dot(gf[...], xg[:, lanes(ch)])
        inner = cubic_term * f32(a2a[:, lanes(ch)]) + quintic_term * inner
        wg[rows(x, c), lanes(ch)] = dot(sel[...], inner.astype(jnp.bfloat16)).astype(jnp.bfloat16)
        gather_start(wg, ch, 1)

    def out_copy(i, k, src, start_col, to):
        off, size = cuts[i]
        return copy(src.at[:, off:off + size],
                    y_ref.at[:, pl.ds(pl.multiple_of(start_col + off, 128), size)],
                    out_s.at[i, k - 1], out_r.at[i, k - 1], to)

    for ch in range(2):
        gather_end(wg, ch, 1)
        yp[:, lanes(ch)] = dot(gf[...], wg[:, lanes(ch)]).astype(jnp.bfloat16)
        for i in ((0,), (1, 2))[ch]:
            off, size = cuts[i]

            def go(i=i, off=off, size=size):
                for k in order:
                    out_copy(i, k, yp.at[block(y + k), :], first(y), ydev[k]).start()
                y_ref[:, pl.ds(pl.multiple_of(first(y) + off, 128), size)] = yp[block(y), off:off + size]
            if i < 2:
                go()
            else:
                pl.when(y % 4 == 3)(go)

    for i in range(3):
        for k in order:
            src = (y - k + NY) % NY

            def got(i=i, k=k, src=src):
                out_copy(i, k, yp.at[block(y), :], first(src), ydev[k]).wait_recv()
            if i < 2:
                got()
            else:
                pl.when(src % 4 == 3)(got)

    for op in pending:
        op.wait_send()
    for i in range(3):
        for k in order:
            t = (y + k) % NY

            def sent(i=i, k=k, t=t):
                off, size = cuts[i]
                copy(xs.at[:, pl.ds(pl.multiple_of(first(t) + off, 128), size)],
                     a2a.at[block(y), off:off + size],
                     in_s.at[i, k - 1], in_r.at[i, k - 1], ydev[k]).wait_send()

            def left(i=i, k=k):
                out_copy(i, k, yp.at[block(y + k), :], first(y), ydev[k]).wait_send()
            if i < 2:
                sent()
                left()
            else:
                pl.when(t % 4 == 3)(sent)
                pl.when(y % 4 == 3)(left)


def on_device(iterate):
    bf = jnp.bfloat16
    dma = pltpu.SemaphoreType.DMA
    applied = pl.pallas_call(
        kernel,
        out_shape=jax.ShapeDtypeStruct((PAD, iterate.shape[1]), bf),
        in_specs=[pl.BlockSpec(memory_space=pltpu.VMEM)],
        out_specs=pl.BlockSpec(memory_space=pltpu.VMEM),
        scratch_shapes=[
            pltpu.VMEM((PAD, iterate.shape[1]), bf),
            pltpu.VMEM((DENSE, TALL), bf),
            pltpu.VMEM((TALL, WIDE), bf),
            pltpu.VMEM((FULL, WIDE), bf),
            pltpu.VMEM((FULL, WIDE), bf),
            pltpu.VMEM((TALL, FULL), bf),
            pltpu.VMEM((2, 4, PAD, FULL), bf),
            pltpu.VMEM((PAD, FULL), bf),
            pltpu.VMEM((PAD, FULL), bf),
            pltpu.VMEM((TALL, FULL), bf),
            pltpu.VMEM((TALL, WIDE), bf),
            dma((3, 7)), dma((3, 7)),
            dma((2, 2, 7)), dma((2, 2, 7)),
            dma((2, 4, 2)), dma((2, 4, 2)),
            dma((2,)), dma((2,)),
            dma((2, 4, 2)), dma((2, 4, 2)),
            dma((3, 7)), dma((3, 7)),
        ],
        compiler_params=pltpu.CompilerParams(
            collective_id=0, has_side_effects=True, vmem_limit_bytes=50 * 2**20),
        name="newton_schulz",
    )(iterate)
    rounded = iterate.astype(bf).astype(jnp.float32)
    return math.sqrt(COLS) * (linear_term * rounded + applied[:OWN].astype(jnp.float32))


def solution(mesh):
    spec = P(("mat", "row"), "col")
    return jax.shard_map(on_device, mesh=mesh, in_specs=(spec,), out_specs=spec, check_vma=False)
```

time: 550 us -> 140 us (0.25)
  waiting for transfers between devices: 428 us -> 0 us
  Pallas kernels: 0 us -> 137 us
  starting transfers between devices: 63.8 us -> 0 us
  local copies, waits for them, and re-layouts: 18.8 us -> 1.22 us
  blocking collectives: 14 us -> 0 us
  matrix products: 11.4 us -> 0 us
  other arithmetic: 11.6 us -> 1.11 us
    ppermute x15 -> x0, waiting for transfers between devices: 428 us -> none  [partner_2(): return lax.ppermute(value, axis, pairs)]
    pallas_call x0 -> x1, Pallas kernels: none -> 137 us  [on_device(): pl.pallas_call(kernel, out_shape=jax.ShapeDtypeStruct((PAD, iterate.shape...]
    ppermute x15 -> x0, starting transfers between devices: 63.8 us -> none  [partner_2(): return lax.ppermute(value, axis, pairs)]
    psum x1 -> x0, blocking collectives: 14 us -> none  [on_device(): gram_tile = lax.psum(partial_value, 'col').astype(jnp.bfloat16)]
    dot_general x4 -> x0, matrix products: 11.4 us -> none  [the longest x3 6.79 us: product(): return jnp.dot(former, latter, preferred_element_type=jnp.float32)]
    reshape x9 -> x0, local copies, waits for them, and re-layouts: 7.62 us -> none  [the longest x1 4.21 us: on_device(): row_tiles = row_tiles.reshape(super_rows, group_size, group_size, -1).tra...]
  transfers between devices with their start and end apart: 15 -> 0, of which waited for: 13 -> 0; matrix products, arithmetic and copies ran while one was open for 3% -> 0% of each run, Pallas kernels for 0% -> 0%
where the time goes in v1:
time: 140 us; the launch traced here: 139 us
  Pallas kernels  137 us (98%)
    pallas_call x1, Pallas kernels, on_device(): pl.pallas_call(kernel, out_shape=jax.ShapeDtypeStruct((PAD, iterate.shape...  137 us

profile of v1, /device:TPU:1, one launch (start us, length us, event | category | flops | bytes accessed | tf_op | source)
XLA Modules:
  0.0 139.4 jit_solution(3025944397256068304)
XLA Ops:
  0.0 0.0 copy-start
  0.0 1.2 copy-done
  1.2 137.1 %newton_schulz.1 = bf16[48,5376]{1,0:T(8,128)(2,1)S(1)} custom-call(f32[42,5376]{1,0:T(8,128)S(1)} %copy-done), custom_call_target="tpu_custom_call" | custom-call | tf_op jit(solution)/shard_map/newton_schulz/pallas_call | solution.py:269
  138.3 1.1 add_multiply_fusion
Async XLA Ops:
  0.0 1.2 copy-start

commit v2 on v0

v2 whole, which is shorter than its diff:
```python
import math

import jax
import jax.numpy as jnp
from jax import lax
from jax.experimental import pallas as pl
from jax.experimental.pallas import tpu as pltpu
from jax.sharding import PartitionSpec as P

COLS = 10752

linear_term = 3.4445
cubic_term = -4.775
quintic_term = 2.0315

NY = 8
NX = 4
NP = 8
OWN = 42
PAD = 48
DENSE = NY * OWN
TALL = NY * PAD
FULL = NP * DENSE
WIDE = 768
CHUNK = 256
CUTS = ((0, 256), (256, 256), (512, 128), (640, 128))
ORDER = (4, 3, 5, 2, 6, 1, 7)
STRIPS = ((0, 384, 0), (384, 256, 1), (640, 640, 1), (1280, 640, 0), (1920, 384, 0), (2304, 384, 1))


def dot(a, b, dims=((1,), (0,))):
    return lax.dot_general(a, b, (dims, ((), ())), preferred_element_type=jnp.float32)


def f32(v):
    return v.astype(jnp.float32)


def bf16(v):
    return v.astype(jnp.bfloat16)


def kernel(x_ref, y_ref, xf, xs, sel, a2a, xg, wg, gp, rb, zs, zr, gf, yp, x_sem,
           in_s, in_r, ag_s, ag_r, rs_s, rs_r, z_s, z_r, gg_s, gg_r, out_s, out_r):
    m, r, z = lax.axis_index("mat"), lax.axis_index("row"), lax.axis_index("col")
    y, p = r // NP, r % NP
    x, c = p // 2, p % 2
    pending = []

    def dev(yy, xx, cc):
        return (m, (yy % NY) * NP + (xx % NX) * 2 + cc, z)

    def copy(src, dst, ssem, rsem, to):
        return pltpu.make_async_remote_copy(
            src_ref=src, dst_ref=dst, send_sem=ssem, recv_sem=rsem,
            device_id=to, device_id_type=pl.DeviceIdType.MESH)

    def send(src, dst, ssem, rsem, to):
        op = copy(src, dst, ssem, rsem, to)
        op.start()
        pending.append(op.wait_send)

    def arrive(dst, ssem, rsem, to):
        copy(dst, dst, ssem, rsem, to).wait_recv()

    def when_whole(i, yy, run):
        if i < 3:
            run()
        else:
            pl.when(yy % 4 == 3)(run)

    def launch(op, i, yy):
        when_whole(i, yy, op.start)
        pending.append(lambda: when_whole(i, yy, op.wait_send))

    def drain():
        for wait in pending:
            wait()
        pending.clear()

    sibling = dev(y, x, 1 - c)
    east, west = dev(y, x + 1, c), dev(y, x + 3, c)
    other_z = (m, r, 1 - z)
    ydev = [dev(y + k, x, c) for k in range(NY)]
    ways = (ydev[1], ydev[NY - 1])
    signs = (1, NY - 1)

    fetch = pltpu.make_async_copy(x_ref, xf, x_sem)
    fetch.start()
    a2a[:, 640:768] = jnp.zeros((TALL, 128), jnp.bfloat16)
    barrier = pltpu.get_barrier_semaphore()
    for to in ydev[1:] + [sibling, east, west, other_z]:
        pl.semaphore_signal(barrier, inc=1, device_id=to, device_id_type=pl.DeviceIdType.MESH)

    row = lax.broadcasted_iota(jnp.int32, (DENSE, TALL), 0)
    col = lax.broadcasted_iota(jnp.int32, (DENSE, TALL), 1)
    place = row
    for k in range(1, NY):
        place = place + jnp.where(row >= OWN * k, PAD - OWN, 0)
    sel[...] = bf16(jnp.where(col == place, 1.0, 0.0))
    fetch.wait()
    xs[32:48, :] = jnp.zeros((16, xs.shape[1]), jnp.bfloat16)
    xs[0:OWN, :] = bf16(xf[...])
    pl.semaphore_wait(barrier, NY + 3)

    def first(yy):
        return pl.multiple_of((21 * yy) // 4 * 128, 128)

    def cut(ref, yy, i):
        off, size = CUTS[i]
        return ref.at[:, pl.ds(pl.multiple_of(first(yy) + off, 128), size)]

    def block(yy):
        return pl.ds(pl.multiple_of((yy % NY) * PAD, 16), PAD)

    def in_copy(i, k, src, dst):
        off, size = CUTS[i]
        return copy(cut(xs, src, i), a2a.at[block(dst), off:off + size],
                    in_s.at[i, k - 1], in_r.at[i, k - 1], ydev[k])

    for i in range(4):
        for k in ORDER:
            launch(in_copy(i, k, (y + k) % NY, y), i, (y + k) % NY)

    for i, (off, size) in enumerate(CUTS):
        def own(i=i, off=off, size=size):
            a2a[block(y), off:off + size] = cut(xs, y, i)[...]
        when_whole(i, y, own)

    def in_wait(i):
        for k in ORDER:
            when_whole(i, y, in_copy(i, k, y, y - k + NY).wait_recv)

    def lanes(ch):
        return slice(ch * CHUNK, (ch + 1) * CHUNK)

    class Gather:
        def __init__(self, buf, n, ch):
            self.buf, self.n, self.ch = buf, n, ch

        def ref(self, place, cc, part=None):
            rows = pl.ds(pl.multiple_of((place * 2 + cc) * DENSE, 16), DENSE)
            lo = self.ch * CHUNK
            if part is None:
                return self.buf.at[rows, lo:lo + CHUNK]
            return self.buf.at[rows, lo + part * 128:lo + part * 128 + 128]

        def push(self, q, src, dst, to):
            send(src, dst, ag_s.at[self.n, self.ch, q], ag_r.at[self.n, self.ch, q], to)

        def wait(self, q, ref):
            arrive(ref, ag_s.at[self.n, self.ch, q], ag_r.at[self.n, self.ch, q], sibling)

        def start(self):
            mine = self.ref(0, c)
            self.push(0, mine, self.ref(1, c), east)
            self.push(1, mine, self.ref(2, c), west)
            self.push(2, mine, mine, sibling)

        def near(self):
            self.wait(0, self.ref(1, c))
            self.push(3, self.ref(1, c, 0), self.ref(3, c, 0), east)
            self.push(5, self.ref(1, c), self.ref(1, c), sibling)
            self.wait(1, self.ref(2, c))
            self.push(4, self.ref(2, c, 1), self.ref(3, c, 1), west)
            self.push(6, self.ref(2, c), self.ref(2, c), sibling)

        def far(self):
            self.wait(3, self.ref(3, c, 0))
            self.wait(4, self.ref(3, c, 1))
            self.push(7, self.ref(3, c), self.ref(3, c), sibling)

        def pair(self):
            self.wait(2, self.ref(0, 1 - c))

        def near_pair(self):
            self.wait(5, self.ref(1, 1 - c))
            self.wait(6, self.ref(2, 1 - c))

        def far_pair(self):
            self.wait(7, self.ref(3, 1 - c))

    gx = [Gather(xg, 0, ch) for ch in range(3)]
    gw = [Gather(wg, 1, ch) for ch in range(3)]

    def share(ch):
        in_wait(ch)
        if ch == 2:
            in_wait(3)
        gx[ch].ref(0, c)[...] = bf16(dot(sel[...], a2a[:, lanes(ch)]))
        gx[ch].start()

    def gram(lo, hi):
        while lo < hi:
            n = min(384, hi - lo)
            gp[:, lo:lo + n] = bf16(dot(a2a[...], xg[lo:lo + n, :], ((1,), (1,))))
            lo += n

    def at(q):
        return slice(STRIPS[q][0], STRIPS[q][0] + STRIPS[q][1])

    def rs_send(q, k, d):
        t = block(y + signs[d] * (4 - k))
        send(gp.at[t, at(q)], rb.at[d, k, :, at(q)], rs_s.at[q, d, k], rs_r.at[q, d, k], ways[d])

    def rs_wait(q, k, d):
        arrive(rb.at[d, k, :, at(q)], rs_s.at[q, d, k], rs_r.at[q, d, k], ways[d])

    def rs_start(*strips):
        for q in strips:
            far = STRIPS[q][2]
            rs_send(q, 0, far)
            rs_send(q, 1, 1 - far)

    def rs_step(k, *strips):
        for q in strips:
            for d in range(2):
                if k == 1 and d != STRIPS[q][2]:
                    continue
                t = block(y + signs[d] * (4 - k))
                rs_wait(q, k - 1, d)
                gp[t, at(q)] = bf16(f32(gp[t, at(q)]) + f32(rb[d, k - 1, :, at(q)]))
                rs_send(q, k, d)

    def rs_end(*strips):
        for q in strips:
            rs_wait(q, 3, 0)
            rs_wait(q, 3, 1)
            zs[:, at(q)] = bf16(f32(gp[block(y), at(q)]) + f32(rb[0, 3, :, at(q)]) + f32(rb[1, 3, :, at(q)]))
            send(zs.at[:, at(q)], zr.at[:, at(q)], z_s.at[q], z_r.at[q], other_z)

    def gg_ref(q, k, d):
        return gf.at[block(y + (NY - signs[d]) * k), at(q)]

    def gg_send(q, k, d):
        send(gg_ref(q, k, d), gg_ref(q, k, d), gg_s.at[q, d, k], gg_r.at[q, d, k], ways[d])

    def gg_wait(q, k, d):
        arrive(gg_ref(q, k + 1, d), gg_s.at[q, d, k], gg_r.at[q, d, k], ways[d])

    def gg_start(*strips):
        for q in strips:
            arrive(zr.at[:, at(q)], z_s.at[q], z_r.at[q], other_z)
            gf[block(y), at(q)] = bf16(f32(zs[:, at(q)]) + f32(zr[:, at(q)]))
            for d in range(2):
                gg_send(q, 0, d)

    def gg_step(k, *strips):
        for q in strips:
            for d in range(2):
                gg_wait(q, k - 1, d)
                if k < 3 or d == STRIPS[q][2]:
                    gg_send(q, k, d)

    def gg_end(*strips):
        for q in strips:
            gg_wait(q, 3, STRIPS[q][2])

    share(0)
    share(1)
    gx[0].near()
    share(2)
    for g in gx:
        g.pair()
    gram(0, 640)
    rs_start(0, 1)
    gx[1].near()
    rs_step(1, 0, 1)
    gx[2].near()
    rs_step(2, 0, 1)
    for g in gx:
        g.near_pair()
    gram(640, 1920)
    rs_start(2, 3)
    rs_step(3, 0, 1)
    for g in gx:
        g.far()
    for g in gx:
        g.far_pair()
    gram(1920, 2688)
    rs_start(4, 5)
    rs_end(0, 1)
    rs_step(1, 2, 3, 4, 5)
    gg_start(0, 1)
    rs_step(2, 2, 3, 4, 5)
    gg_step(1, 0, 1)
    rs_step(3, 2, 3, 4, 5)
    gg_step(2, 0, 1)
    rs_end(2, 3, 4, 5)
    gg_step(3, 0, 1)
    gg_start(2, 3, 4, 5)
    gg_step(1, 2, 3, 4, 5)
    gg_step(2, 2, 3, 4, 5)
    gg_step(3, 2, 3, 4, 5)
    gg_end(0, 1, 2, 3, 4, 5)

    for ch in range(3):
        inner = cubic_term * f32(a2a[:, lanes(ch)]) + quintic_term * dot(gf[...], xg[:, lanes(ch)])
        gw[ch].ref(0, c)[...] = bf16(dot(sel[...], bf16(inner)))
        gw[ch].start()

    def out_copy(i, k, src, dst):
        off, size = CUTS[i]
        return copy(yp.at[block(dst), off:off + size], cut(y_ref, src, i),
                    out_s.at[i, k - 1], out_r.at[i, k - 1], ydev[k])

    drain()
    for g in gw:
        g.near()
    for ch in range(3):
        gw[ch].far()
        gw[ch].pair()
        gw[ch].near_pair()
        gw[ch].far_pair()
        yp[:, lanes(ch)] = bf16(dot(gf[...], wg[:, lanes(ch)]))
        for i in ((0,), (1,), (2, 3))[ch]:
            for k in ORDER:
                launch(out_copy(i, k, y, y + k), i, y)

            def own(i=i):
                cut(y_ref, y, i)[...] = yp[block(y), CUTS[i][0]:CUTS[i][0] + CUTS[i][1]]
            when_whole(i, y, own)

    for i in range(4):
        for k in ORDER:
            src = (y - k + NY) % NY
            when_whole(i, src, out_copy(i, k, src, y).wait_recv)
    drain()


def on_device(iterate):
    bf = jnp.bfloat16
    dma = pltpu.SemaphoreType.DMA
    local = iterate.shape[1]
    n = len(STRIPS)
    applied = pl.pallas_call(
        kernel,
        out_shape=jax.ShapeDtypeStruct((PAD, local), bf),
        in_specs=[pl.BlockSpec(memory_space=pl.ANY)],
        out_specs=pl.BlockSpec(memory_space=pltpu.VMEM),
        scratch_shapes=[
            pltpu.VMEM((OWN, local), jnp.float32),
            pltpu.VMEM((PAD, local), bf),
            pltpu.VMEM((DENSE, TALL), bf),
            pltpu.VMEM((TALL, WIDE), bf),
            pltpu.VMEM((FULL, WIDE), bf),
            pltpu.VMEM((FULL, WIDE), bf),
            pltpu.VMEM((TALL, FULL), bf),
            pltpu.VMEM((2, 4, PAD, FULL), bf),
            pltpu.VMEM((PAD, FULL), bf),
            pltpu.VMEM((PAD, FULL), bf),
            pltpu.VMEM((TALL, FULL), bf),
            pltpu.VMEM((TALL, WIDE), bf),
            dma,
            dma((4, 7)), dma((4, 7)),
            dma((2, 3, 8)), dma((2, 3, 8)),
            dma((n, 2, 4)), dma((n, 2, 4)),
            dma((n,)), dma((n,)),
            dma((n, 2, 4)), dma((n, 2, 4)),
            dma((4, 7)), dma((4, 7)),
        ],
        compiler_params=pltpu.CompilerParams(
            collective_id=0, has_side_effects=True, vmem_limit_bytes=50 * 2**20),
        name="newton_schulz",
    )(iterate)
    rounded = f32(iterate.astype(bf))
    return math.sqrt(COLS) * (linear_term * rounded + f32(applied[:OWN]))


def solution(mesh):
    spec = P(("mat", "row"), "col")
    return jax.shard_map(on_device, mesh=mesh, in_specs=(spec,), out_specs=spec, check_vma=False)
```

time: 550 us -> 117 us (0.21)
  waiting for transfers between devices: 428 us -> 0 us
  Pallas kernels: 0 us -> 115 us
  starting transfers between devices: 63.8 us -> 0 us
  local copies, waits for them, and re-layouts: 18.8 us -> 1.22 us
  blocking collectives: 14 us -> 0 us
  matrix products: 11.4 us -> 0 us
  other arithmetic: 11.6 us -> 1.11 us
    ppermute x15 -> x0, waiting for transfers between devices: 428 us -> none  [partner_2(): return lax.ppermute(value, axis, pairs)]
    pallas_call x0 -> x1, Pallas kernels: none -> 115 us  [on_device(): pl.pallas_call(kernel, out_shape=jax.ShapeDtypeStruct((PAD, local), bf),...]
    ppermute x15 -> x0, starting transfers between devices: 63.8 us -> none  [partner_2(): return lax.ppermute(value, axis, pairs)]
    psum x1 -> x0, blocking collectives: 14 us -> none  [on_device(): gram_tile = lax.psum(partial_value, 'col').astype(jnp.bfloat16)]
    dot_general x4 -> x0, matrix products: 11.4 us -> none  [the longest x3 6.79 us: product(): return jnp.dot(former, latter, preferred_element_type=jnp.float32)]
    reshape x9 -> x0, local copies, waits for them, and re-layouts: 7.62 us -> none  [the longest x1 4.21 us: on_device(): row_tiles = row_tiles.reshape(super_rows, group_size, group_size, -1).tra...]
  transfers between devices with their start and end apart: 15 -> 0, of which waited for: 13 -> 0; matrix products, arithmetic and copies ran while one was open for 3% -> 0% of each run, Pallas kernels for 0% -> 0%
where the time goes in v2:
time: 117 us
  Pallas kernels  115 us (98%)
  local copies, waits for them, and re-layouts  1.22 us (1%)
    pallas_call x1, Pallas kernels, on_device(): pl.pallas_call(kernel, out_shape=jax.ShapeDtypeStruct((PAD, local), bf),...  115 us

profile of v2, /device:TPU:1, one launch (start us, length us, event | category | flops | bytes accessed | tf_op | source)
XLA Modules:
  0.0 117.3 jit_solution(6990219984555750222)
XLA Ops:
  0.0 0.0 copy-start
  0.0 1.2 %copy-done = f32[42,5376]{1,0:T(8,128)S(1)} copy-done((f32[42,5376]{1,0:T(8,128)S(1)}, f32[42,5376]{1,0:T(8,128)}, u32[]{:S(2)}) %copy-start) | copy-done | bytes 903192
  1.2 115.0 %newton_schulz.1 = bf16[48,5376]{1,0:T(8,128)(2,1)S(1)} custom-call(f32[42,5376]{1,0:T(8,128)S(1)} %copy-done), custom_call_target="tpu_custom_call" | custom-call | tf_op jit(solution)/shard_map/newton_schulz/pallas_call | solution.py:336
  116.2 1.1 add_multiply_fusion
Async XLA Ops:
  0.0 1.2 %copy-start = (f32[42,5376]{1,0:T(8,128)S(1)}, f32[42,5376]{1,0:T(8,128)}, u32[]{:S(2)}) copy-start(f32[42,5376]{1,0:T(8,128)} %x_ref.1) | copy-start | bytes 2709508

commit v3 on v2

v3 whole, which is shorter than its diff:
```python
import math

import jax
import jax.numpy as jnp
from jax import lax
from jax.experimental import pallas as pl
from jax.experimental.pallas import tpu as pltpu
from jax.sharding import PartitionSpec as P

COLS = 10752

linear_term = 3.4445
cubic_term = -4.775
quintic_term = 2.0315

NY = 8
NX = 4
NP = 8
OWN = 42
PAD = 48
DENSE = NY * OWN
SLOT = NY * PAD
WIDE = 768
CUTS = ((0, 128), (128, 256), (384, 256), (640, 128))
ORDER = (4, 3, 5, 2, 6, 1, 7)
UP, DOWN_PAIR, FAR, DOWN, UP_PAIR = 2, 3, 4, 5, 6
BLOCKS = 5
SUM = BLOCKS * SLOT
STRIPS = (
    (0, 768, 0, 0, False),
    (768, 384, 1, 2, True),
    (1152, 384, 0, 3, True),
    (1536, 384, 1, 4, True),
)


def dot(a, b, dims=((1,), (0,))):
    return lax.dot_general(a, b, (dims, ((), ())), preferred_element_type=jnp.float32)


def f32(v):
    return v.astype(jnp.float32)


def bf16(v):
    return v.astype(jnp.bfloat16)


def kernel(x_ref, y_ref, xs, sel, unsel, eye, a2a, xg, wg, gp, rb, zs, zr, gf, mx, gl, yp,
           in_s, in_r, ag_s, ag_r, rs_s, rs_r, z_s, z_r, gg_s, gg_r, mx_s, mx_r, out_s, out_r):
    m, r, z = lax.axis_index("mat"), lax.axis_index("row"), lax.axis_index("col")
    y, p = r // NP, r % NP
    x, c = p // 2, p % 2
    pending = []

    def dev(yy, xx, cc):
        return (m, (yy % NY) * NP + (xx % NX) * 2 + cc, z)

    def copy(src, dst, ssem, rsem, to):
        return pltpu.make_async_remote_copy(
            src_ref=src, dst_ref=dst, send_sem=ssem, recv_sem=rsem,
            device_id=to, device_id_type=pl.DeviceIdType.MESH)

    def send(src, dst, ssem, rsem, to):
        copy(src, dst, ssem, rsem, to).start()

    def arrive(ref, rsem):
        copy(ref, ref, rsem, rsem, sibling).wait_recv()

    def leave(ref, ssem):
        pending.append(copy(ref, ref, ssem, ssem, sibling).wait_send)

    def when_whole(i, yy, run):
        if i < 3:
            run()
        else:
            pl.when(yy % 4 == 3)(run)

    def whole(i, width, buf, act):
        if i < 3:
            act(buf.at[0:(NY - 1) * PAD, 0:width])()
        else:
            pl.when(y % 4 == 3)(act(buf.at[0:PAD, 0:width]))
            pl.when(y % 4 != 3)(act(buf.at[0:2 * PAD, 0:width]))

    def one(i, width, buf, act):
        when_whole(i, y, act(buf.at[0:(NY - 1) * PAD, 0:width]))

    def drain():
        for wait in pending:
            wait()
        pending.clear()

    sibling = dev(y, x, 1 - c)
    east, west = dev(y, x + 1, c), dev(y, x + 3, c)
    other_z = (m, r, 1 - z)
    ydev = [dev(y + k, x, c) for k in range(NY)]
    ways = (ydev[1], ydev[NY - 1])
    signs = (1, NY - 1)
    far_core = (c + x // 2) % 2
    partners = (east, dev(y, x + 3, 1 - c), dev(y, x + 2, far_core))
    mirrors = (west, dev(y, x + 1, 1 - c), dev(y, x + 2, 1 - far_core))

    a2a[:, 640:768] = jnp.zeros((SLOT, 128), jnp.bfloat16)
    barrier = pltpu.get_barrier_semaphore()
    greet = ydev[1:] + [sibling, east, west, other_z, partners[1], partners[2], mirrors[1], mirrors[2]]
    for to in greet:
        pl.semaphore_signal(barrier, inc=1, device_id=to, device_id_type=pl.DeviceIdType.MESH)

    xs[32:48, :] = jnp.zeros((16, xs.shape[1]), jnp.bfloat16)
    xs[0:OWN, :] = bf16(x_ref[...])
    pl.semaphore_wait(barrier, len(greet))

    def first(yy):
        return pl.multiple_of((21 * yy) // 4 * 128, 128)

    def cut(ref, yy, i):
        off, size = CUTS[i]
        return ref.at[:, pl.ds(pl.multiple_of(first(yy) + off, 128), size)]

    def block(yy):
        return pl.ds(pl.multiple_of((yy % NY) * PAD, 16), PAD)

    def in_copy(i, k, src, dst):
        off, size = CUTS[i]
        return copy(cut(xs, src, i), a2a.at[block(dst), off:off + size],
                    in_s.at[i], in_r.at[i], ydev[k])

    for i in range(4):
        for k in ORDER:
            when_whole(i, (y + k) % NY, in_copy(i, k, (y + k) % NY, y).start)
        pending.append(lambda i=i: whole(i, CUTS[i][1], a2a, lambda ref: copy(ref, ref, in_s.at[i], in_s.at[i], sibling).wait_send))

    for i, (off, size) in enumerate(CUTS):
        def own(i=i, off=off, size=size):
            a2a[block(y), off:off + size] = cut(xs, y, i)[...]
        when_whole(i, y, own)

    row = lax.broadcasted_iota(jnp.int32, (SLOT, SLOT), 0)
    col = lax.broadcasted_iota(jnp.int32, (SLOT, SLOT), 1)

    def spread(v):
        place = v
        for k in range(1, NY):
            place = place + jnp.where(v >= OWN * k, PAD - OWN, 0)
        return jnp.where(v < DENSE, place, -1)
    sel[...] = bf16(jnp.where(col == spread(row), 1.0, 0.0))
    unsel[...] = bf16(jnp.where(row == spread(col), 1.0, 0.0))
    eye[...] = bf16(jnp.where(row == col, 1.0, 0.0))
    for s in range(NP):
        xg[s * SLOT + DENSE:(s + 1) * SLOT, :] = jnp.zeros((SLOT - DENSE, WIDE), jnp.bfloat16)
        wg[s * SLOT + DENSE:(s + 1) * SLOT, :] = jnp.zeros((SLOT - DENSE, WIDE), jnp.bfloat16)

    def in_wait(i):
        one(i, CUTS[i][1], a2a, lambda ref: copy(ref, ref, in_r.at[i], in_r.at[i], sibling).wait_recv)

    def lanes(ch):
        return slice(CUTS[ch][0], CUTS[ch][0] + CUTS[ch][1])

    class Gather:
        def __init__(self, buf, n, ch):
            self.buf, self.n, self.ch = buf, n, ch

        def ref(self, slot, part=None):
            lo, size = ((0, DENSE), (0, 176), (176, 160))[0 if part is None else part + 1]
            return self.buf.at[pl.ds(pl.multiple_of(slot * SLOT + lo, 16), size), lanes(self.ch)]

        def far(self, xx):
            return FAR + 3 * ((xx % NX) // 2)

        def push(self, q, src, dst, to):
            rsem = ag_r.at[self.n, 0 if q > 2 and self.n == 0 else self.ch, q]
            send(src, dst, ag_s.at[self.n, self.ch], rsem, to)

        def wait(self, q, ref):
            arrive(ref, ag_r.at[self.n, self.ch, q])

        def start(self):
            mine = self.ref(c)
            self.push(0, mine, self.ref(DOWN), east)
            self.push(1, mine, self.ref(UP), west)
            self.push(3, mine, mine, sibling)
            if self.ch == 3:
                self.push(2, mine, self.ref(self.far(x + 2)), dev(y, x + 2, c))

        def near(self):
            self.wait(0, self.ref(DOWN))
            if self.ch < 3:
                self.push(2, self.ref(DOWN, 0), self.ref(self.far(x + 1), 0), east)
            self.push(4, self.ref(DOWN), self.ref(DOWN_PAIR), sibling)
            self.wait(1, self.ref(UP))
            if self.ch < 3:
                self.push(2, self.ref(UP, 1), self.ref(self.far(x + 3), 1), west)
            self.push(4, self.ref(UP), self.ref(UP_PAIR), sibling)

        def beyond(self):
            self.wait(2, self.ref(self.far(x)))
            self.push(5, self.ref(self.far(x)), self.ref(2 * FAR + 3 - self.far(x)), sibling)
            leave(self.buf.at[0:7 * DENSE, lanes(self.ch)], ag_s.at[self.n, self.ch])

        def pairs(self):
            for q, rows in ((3, 1), (4, 2), (5, 1)):
                self.wait(q, self.buf.at[0:rows * DENSE, lanes(self.ch)])

    gx = [Gather(xg, 0, ch) for ch in range(4)]
    gw = [Gather(wg, 1, ch) for ch in range(4)]

    def pairs(q):
        arrive(xg.at[0:(2 if q == 4 else 1) * DENSE, :], ag_r.at[0, 0, q])

    def mine(buf, ch):
        return buf.at[pl.ds(pl.multiple_of(c * SLOT, 16), SLOT), lanes(ch)]

    def share(ch):
        in_wait(ch)
        mine(xg, ch)[...] = bf16(dot(sel[...], a2a[:, lanes(ch)]))
        gx[ch].start()

    def gram(b):
        at = slice(b * SLOT, (b + 1) * SLOT)
        gp[:, at] = bf16(dot(a2a[...], xg[at, :], ((1,), (1,))))

    def at(q):
        return slice(STRIPS[q][0], STRIPS[q][0] + STRIPS[q][1])

    def rs_send(q, slot, t, k, to):
        send(gp.at[block(t), at(q)], rb.at[slot, :, at(q)], rs_s.at[q], rs_r.at[q, k], to)

    def rs_wait(q, k, n):
        arrive(rb.at[0:n, :, at(q)], rs_r.at[q, k])

    def add(t, q, *slots):
        v = f32(gp[block(t), at(q)])
        for slot in slots:
            v = v + f32(rb[slot, :, at(q)])
        return bf16(v)

    def rs_start(q):
        far = STRIPS[q][2]
        leave(gp.at[0:(NY - 1) * PAD, at(q)], rs_s.at[q])
        if STRIPS[q][4]:
            rs_send(q, 0, y + signs[far] * 4, 0, ydev[2 * signs[far] % NY])
            for d in range(2):
                rs_send(q, 1 + d, y + signs[d] * 3, 0, ways[d])
            for d in range(2):
                rs_send(q, 5 + d, y + signs[d], 1, ways[d])
        else:
            rs_send(q, 4 * far, y + 4, 0, ways[far])
            rs_send(q, 4 * (1 - far) + 1, y + signs[1 - far] * 3, 1, ways[1 - far])

    def rs_step(q, k):
        far = STRIPS[q][2]
        if STRIPS[q][4]:
            rs_wait(q, 0, 3)
            for d in (far, 1 - far):
                t = y + signs[d] * 2
                gp[block(t), at(q)] = add(t, q, 1 + d, 0) if d == far else add(t, q, 1 + d)
                rs_send(q, 3 + d, t, 1, ydev[2 * signs[d] % NY])
            return
        rs_wait(q, k - 1, 1 if k == 1 else 2)
        for d in range(2):
            if k == 1 and d != far:
                continue
            t = y + signs[d] * (4 - k)
            gp[block(t), at(q)] = add(t, q, 4 * d + k - 1)
            rs_send(q, 4 * d + k, t, k, ways[d])

    def rs_end(q):
        if STRIPS[q][4]:
            rs_wait(q, 1, 4)
            zs[:, at(q)] = add(y, q, 3, 4, 5, 6)
        else:
            rs_wait(q, 3, 2)
            zs[:, at(q)] = add(y, q, 3, 7)
        send(zs.at[:, at(q)], zr.at[:, at(q)], z_s.at[q], z_r.at[q], other_z)
        leave(zs.at[:, at(q)], z_s.at[q])

    def mirror(q, j):
        b = STRIPS[q][3] - UP
        if b >= 0:
            send(gf.at[block(y + j), at(q)], mx.at[b, block(y + j), :], mx_s.at[b], mx_r.at[b], partners[b])

    def gg_send(q, j, k, to):
        ref = gf.at[block(y + j), at(q)]
        send(ref, ref, gg_s.at[q], gg_r.at[q, k], to)

    def gg_wait(q, k, n):
        arrive(gf.at[0:n * PAD, at(q)], gg_r.at[q, k])

    def gg_start(q):
        arrive(zr.at[:, at(q)], z_r.at[q])
        gf[block(y), at(q)] = bf16(f32(zs[:, at(q)]) + f32(zr[:, at(q)]))
        leave(gf.at[0:(NY - 1) * PAD, at(q)], gg_s.at[q])
        for d in range(2):
            if STRIPS[q][4]:
                gg_send(q, 0, 0, ydev[2 * signs[d] % NY])
            gg_send(q, 0, 0, ways[d])
        mirror(q, 0)
        if STRIPS[q][3] >= UP:
            b = STRIPS[q][3] - UP
            leave(gf.at[:, at(q)], mx_s.at[b])

    def gg_step(q, k):
        far = STRIPS[q][2]
        if STRIPS[q][4]:
            gg_wait(q, 0, 4)
            for d in range(2):
                back = NY - signs[d] * 2 % NY
                if d == far:
                    gg_send(q, back, 1, ydev[2 * signs[d] % NY])
                gg_send(q, back, 1, ways[d])
            for j in (1, NY - 1, 2, NY - 2):
                mirror(q, j)
            return
        gg_wait(q, k - 1, 2)
        for d in range(2):
            back = NY - signs[d] * k % NY
            if k < 3 or d == far:
                gg_send(q, back, k, ways[d])
            mirror(q, back)

    def gg_end(q):
        if STRIPS[q][4]:
            gg_wait(q, 1, 3)
            for j in (3, NY - 3, 4):
                mirror(q, j)
        else:
            gg_wait(q, 3, 1)
            mirror(q, 4)

    def mirror_wait(b):
        arrive(mx.at[b], mx_r.at[b])

    def settle(b):
        at = slice(b * SLOT, (b + 1) * SLOT)
        if b < BLOCKS:
            gl[:, at] = bf16(dot(sel[...], gf[:, at]))
        else:
            turned = bf16(dot(eye[...], mx[b - BLOCKS], ((1,), (1,))))
            gl[:, at] = bf16(dot(turned, sel[...], ((1,), (1,))))

    A, B, C, D = range(4)
    share(0)
    share(1)
    gx[0].near()
    share(2)
    gx[1].near()
    share(3)
    pairs(3)
    gram(0)
    gram(1)
    rs_start(A)
    gx[2].near()
    gx[0].beyond()
    rs_step(A, 1)
    gx[3].near()
    gram(2)
    rs_start(B)
    gx[1].beyond()
    rs_step(A, 2)
    pairs(4)
    gram(3)
    rs_start(C)
    gx[2].beyond()
    gx[3].beyond()
    rs_step(A, 3)
    rs_step(B, 1)
    pairs(5)
    gram(4)
    rs_start(D)
    rs_step(C, 1)
    rs_end(A)
    rs_end(B)
    rs_step(D, 1)
    gg_start(A)
    rs_end(C)
    gg_start(B)
    rs_end(D)
    gg_step(A, 1)
    gg_start(C)
    gg_step(B, 1)
    gg_start(D)
    gg_step(A, 2)
    gg_step(C, 1)
    gg_end(B)
    gg_step(D, 1)
    gg_step(A, 3)
    settle(2)
    gg_end(C)
    settle(3)
    gg_end(D)
    gg_end(A)
    settle(4)
    settle(0)
    settle(1)
    for b in range(3):
        mirror_wait(b)
        settle(BLOCKS + b)

    def inner(ch):
        v = cubic_term * f32(mine(xg, ch)[...]) + quintic_term * dot(gl[...], xg[:, lanes(ch)])
        mine(wg, ch)[...] = bf16(v)
        gw[ch].start()

    def out_copy(i, k, src, dst):
        off, size = CUTS[i]
        return copy(yp.at[block(dst), off:off + size], cut(y_ref, src, i),
                    out_s.at[i], out_r.at[i], ydev[k])

    def outer(ch):
        gw[ch].pairs()
        yp[:, lanes(ch)] = bf16(dot(unsel[...], bf16(dot(gl[...], wg[:, lanes(ch)]))))
        for k in ORDER:
            when_whole(ch, y, out_copy(ch, k, y, y + k).start)
        pending.append(lambda: one(ch, CUTS[ch][1], yp, lambda ref: copy(ref, ref, out_s.at[ch], out_s.at[ch], sibling).wait_send))

        def own():
            cut(y_ref, y, ch)[...] = yp[block(y), lanes(ch)]
        when_whole(ch, y, own)

    inner(0)
    inner(1)
    drain()
    gw[0].near()
    inner(2)
    gw[1].near()
    gw[0].beyond()
    inner(3)
    gw[2].near()
    outer(0)
    gw[1].beyond()
    gw[3].near()
    outer(1)
    gw[2].beyond()
    gw[3].beyond()
    outer(2)
    outer(3)
    for i in range(4):
        whole(i, CUTS[i][1], yp, lambda ref: copy(ref, ref, out_r.at[i], out_r.at[i], sibling).wait_recv)
    drain()


def on_device(iterate):
    bf = jnp.bfloat16
    dma = pltpu.SemaphoreType.DMA
    local = iterate.shape[1]
    n = len(STRIPS)
    applied = pl.pallas_call(
        kernel,
        out_shape=jax.ShapeDtypeStruct((PAD, local), bf),
        in_specs=[pl.BlockSpec(memory_space=pltpu.VMEM)],
        out_specs=pl.BlockSpec(memory_space=pltpu.VMEM),
        scratch_shapes=[
            pltpu.VMEM((PAD, local), bf),
            pltpu.VMEM((SLOT, SLOT), bf),
            pltpu.VMEM((SLOT, SLOT), bf),
            pltpu.VMEM((SLOT, SLOT), bf),
            pltpu.VMEM((SLOT, WIDE), bf),
            pltpu.VMEM((NP * SLOT, WIDE), bf),
            pltpu.VMEM((NP * SLOT, WIDE), bf),
            pltpu.VMEM((SLOT, SUM), bf),
            pltpu.VMEM((8, PAD, SUM), bf),
            pltpu.VMEM((PAD, SUM), bf),
            pltpu.VMEM((PAD, SUM), bf),
            pltpu.VMEM((SLOT, SUM), bf),
            pltpu.VMEM((3, SLOT, SLOT), bf),
            pltpu.VMEM((SLOT, NP * SLOT), bf),
            pltpu.VMEM((SLOT, WIDE), bf),
            dma((4,)), dma((4,)),
            dma((2, 4)), dma((2, 4, 6)),
            dma((n,)), dma((n, 4)),
            dma((n,)), dma((n,)),
            dma((n,)), dma((n, 4)),
            dma((3,)), dma((3,)),
            dma((4,)), dma((4,)),
        ],
        compiler_params=pltpu.CompilerParams(
            collective_id=0, has_side_effects=True, vmem_limit_bytes=50 * 2**20),
        name="newton_schulz",
    )(iterate)
    rounded = f32(iterate.astype(bf))
    return math.sqrt(COLS) * (linear_term * rounded + f32(applied[:OWN]))


def solution(mesh):
    spec = P(("mat", "row"), "col")
    return jax.shard_map(on_device, mesh=mesh, in_specs=(spec,), out_specs=spec, check_vma=False)
```

time: 117 us -> 110 us (0.940)
  Pallas kernels: 115 us -> 108 us
    pallas_call x1, Pallas kernels: 115 us -> 108 us  [on_device(): pl.pallas_call(kernel, out_shape=jax.ShapeDtypeStruct((PAD, local), bf),...]
where the time goes in v3:
time: 110 us
  Pallas kernels  108 us (98%)
  local copies, waits for them, and re-layouts  1.22 us (1%)
  other arithmetic  1.11 us (1%)
    pallas_call x1, Pallas kernels, on_device(): pl.pallas_call(kernel, out_shape=jax.ShapeDtypeStruct((PAD, local), bf),...  108 us

profile of v3, /device:TPU:1, one launch (start us, length us, event | category | flops | bytes accessed | tf_op | source)
XLA Modules:
  0.0 110.0 jit_solution(844979443314388349)
XLA Ops:
  0.0 0.0 copy-start
  0.0 1.2 %copy-done = f32[42,5376]{1,0:T(8,128)S(1)} copy-done((f32[42,5376]{1,0:T(8,128)S(1)}, f32[42,5376]{1,0:T(8,128)}, u32[]{:S(2)}) %copy-start) | copy-done | bytes 903192
  1.2 107.6 %newton_schulz.1 = bf16[48,5376]{1,0:T(8,128)(2,1)S(1)} custom-call(f32[42,5376]{1,0:T(8,128)S(1)} %copy-done), custom_call_target="tpu_custom_call" | custom-call | tf_op jit(solution)/shard_map/newton_schulz/pallas_call | solution.py:448
  108.9 1.1 %add_multiply_fusion = f32[42,5376]{1,0:T(8,128)} fusion(bf16[48,5376]{1,0:T(8,128)(2,1)S(1)} %newton_schulz.1, f32[42,5376]{1,0:T(8,128)S(1)} %copy-done), kind=kLoop, calls=%fused_computation | loop fusion | flops 1354752 | bytes 2257920 | tf_op jit(solution)/shard_map/mul | solution.py:482
Async XLA Ops:
  0.0 1.2 %copy-start = (f32[42,5376]{1,0:T(8,128)S(1)}, f32[42,5376]{1,0:T(8,128)}, u32[]{:S(2)}) copy-start(f32[42,5376]{1,0:T(8,128)} %x_ref.1) | copy-start | bytes 2709508

commit v4 on v3

--- a/solution.py
+++ b/solution.py
@@ -27,11 +27,12 @@
 BLOCKS = 5
 SUM = BLOCKS * SLOT
 STRIPS = (
-    (0, 768, 0, 0, False),
+    (0, 768, 0, 0, True),
     (768, 384, 1, 2, True),
     (1152, 384, 0, 3, True),
     (1536, 384, 1, 4, True),
 )
+GROUPS = ((0, 0, False, True), (768, 1, True, True), (1536, 1, True, False))
 
 
 def dot(a, b, dims=((1,), (0,))):
@@ -47,7 +48,7 @@
 
 
 def kernel(x_ref, y_ref, xs, sel, unsel, eye, a2a, xg, wg, gp, rb, zs, zr, gf, mx, gl, yp,
-           in_s, in_r, ag_s, ag_r, rs_s, rs_r, z_s, z_r, gg_s, gg_r, mx_s, mx_r, out_s, out_r):
+           in_s, in_r, ag_s, ag_r, rs_s, rs_r, z_s, z_r, gg_s, gg_r, zf_s, zf_r, mx_s, mx_r, out_s, out_r):
     m, r, z = lax.axis_index("mat"), lax.axis_index("row"), lax.axis_index("col")
     y, p = r // NP, r % NP
     x, c = p // 2, p % 2
@@ -272,61 +273,86 @@
         else:
             rs_wait(q, 3, 2)
             zs[:, at(q)] = add(y, q, 3, 7)
-        send(zs.at[:, at(q)], zr.at[:, at(q)], z_s.at[q], z_r.at[q], other_z)
-        leave(zs.at[:, at(q)], z_s.at[q])
-
-    def mirror(q, j):
-        b = STRIPS[q][3] - UP
-        if b >= 0:
-            send(gf.at[block(y + j), at(q)], mx.at[b, block(y + j), :], mx_s.at[b], mx_r.at[b], partners[b])
-
-    def gg_send(q, j, k, to):
-        ref = gf.at[block(y + j), at(q)]
-        send(ref, ref, gg_s.at[q], gg_r.at[q, k], to)
-
-    def gg_wait(q, k, n):
-        arrive(gf.at[0:n * PAD, at(q)], gg_r.at[q, k])
-
-    def gg_start(q):
-        arrive(zr.at[:, at(q)], z_r.at[q])
-        gf[block(y), at(q)] = bf16(f32(zs[:, at(q)]) + f32(zr[:, at(q)]))
-        leave(gf.at[0:(NY - 1) * PAD, at(q)], gg_s.at[q])
+
+    def gat(g, side):
+        lo, _, _, shared = GROUPS[g]
+        return pl.ds(pl.multiple_of(lo + side * SLOT, 128), SLOT) if shared else slice(lo, lo + SLOT)
+
+    def z_send(g):
+        theirs = gat(g, 1 - z)
+        send(zs.at[:, theirs], zr.at[:, theirs], z_s.at[g], z_r.at[g], other_z)
+        leave(zs.at[:, 0:SLOT], z_s.at[g])
+
+    def mirror(g, j, side):
+        ref = gf.at[block(y + j), gat(g, side)]
+        if g == 1:
+            i = (side - z) % 2
+            send(ref, mx.at[side, block(y + j), :], mx_s.at[i], mx_r.at[i], dev(y, x + 1 + 2 * side, (c + side) % 2))
+        elif g == 2:
+            send(ref, mx.at[2, block(y + j), :], mx_s.at[2], mx_r.at[2], partners[2])
+
+    def spread_on(g, k, *js):
+        for j in js:
+            if GROUPS[g][3]:
+                ref = gf.at[block(y + j), gat(g, z)]
+                send(ref, ref, zf_s.at[g], zf_r.at[g, k], other_z)
+            mirror(g, j, z)
+
+    def zf_wait(g, k, *js):
+        arrive(gf.at[0:len(js) * PAD, 0:SLOT], zf_r.at[g, k])
+        for j in js:
+            mirror(g, j, 1 - z)
+
+    def gg_send(g, j, k, to):
+        ref = gf.at[block(y + j), gat(g, z)]
+        send(ref, ref, gg_s.at[g], gg_r.at[g, k], to)
+
+    def gg_wait(g, k, n):
+        arrive(gf.at[0:n * PAD, 0:SLOT], gg_r.at[g, k])
+
+    def gg_start(g):
+        here = gat(g, z)
+        arrive(zr.at[:, 0:SLOT], z_r.at[g])
+        gf[block(y), here] = bf16(f32(zs[:, here]) + f32(zr[:, here]))
+        leave(gf.at[0:(NY - 1) * PAD, 0:SLOT], gg_s.at[g])
         for d in range(2):
-            if STRIPS[q][4]:
-                gg_send(q, 0, 0, ydev[2 * signs[d] % NY])
-            gg_send(q, 0, 0, ways[d])
-        mirror(q, 0)
-        if STRIPS[q][3] >= UP:
-            b = STRIPS[q][3] - UP
-            leave(gf.at[:, at(q)], mx_s.at[b])
-
-    def gg_step(q, k):
-        far = STRIPS[q][2]
-        if STRIPS[q][4]:
-            gg_wait(q, 0, 4)
+            if GROUPS[g][2]:
+                gg_send(g, 0, 0, ydev[2 * signs[d] % NY])
+            gg_send(g, 0, 0, ways[d])
+        spread_on(g, 0, 0)
+        if GROUPS[g][3]:
+            leave(gf.at[:, 0:SLOT], zf_s.at[g])
+        if g == 1:
+            leave(gf.at[:, 0:SLOT], mx_s.at[0])
+            leave(gf.at[:, 0:SLOT], mx_s.at[1])
+        elif g == 2:
+            leave(gf.at[:, 0:SLOT], mx_s.at[2])
+
+    def gg_step(g, k):
+        far = GROUPS[g][1]
+        if GROUPS[g][2]:
+            gg_wait(g, 0, 4)
             for d in range(2):
                 back = NY - signs[d] * 2 % NY
                 if d == far:
-                    gg_send(q, back, 1, ydev[2 * signs[d] % NY])
-                gg_send(q, back, 1, ways[d])
-            for j in (1, NY - 1, 2, NY - 2):
-                mirror(q, j)
+                    gg_send(g, back, 1, ydev[2 * signs[d] % NY])
+                gg_send(g, back, 1, ways[d])
+            spread_on(g, 0, 1, NY - 1, 2, NY - 2)
             return
-        gg_wait(q, k - 1, 2)
+        gg_wait(g, k - 1, 2)
         for d in range(2):
             back = NY - signs[d] * k % NY
             if k < 3 or d == far:
-                gg_send(q, back, k, ways[d])
-            mirror(q, back)
-
-    def gg_end(q):
-        if STRIPS[q][4]:
-            gg_wait(q, 1, 3)
-            for j in (3, NY - 3, 4):
-                mirror(q, j)
+                gg_send(g, back, k, ways[d])
+            spread_on(g, 0, back)
+
+    def gg_end(g):
+        if GROUPS[g][2]:
+            gg_wait(g, 1, 3)
+            spread_on(g, 1, 3, NY - 3, 4)
         else:
-            gg_wait(q, 3, 1)
-            mirror(q, 4)
+            gg_wait(g, 3, 1)
+            spread_on(g, 0, 4)
 
     def mirror_wait(b):
         arrive(mx.at[b], mx_r.at[b])
@@ -342,60 +368,62 @@
     A, B, C, D = range(4)
     share(0)
     share(1)
+    share(2)
     gx[0].near()
-    share(2)
+    share(3)
     gx[1].near()
-    share(3)
     pairs(3)
     gram(0)
     gram(1)
     rs_start(A)
     gx[2].near()
     gx[0].beyond()
-    rs_step(A, 1)
     gx[3].near()
     gram(2)
     rs_start(B)
+    rs_step(A, 1)
     gx[1].beyond()
-    rs_step(A, 2)
     pairs(4)
     gram(3)
     rs_start(C)
     gx[2].beyond()
     gx[3].beyond()
-    rs_step(A, 3)
+    rs_end(A)
+    z_send(0)
     rs_step(B, 1)
     pairs(5)
     gram(4)
     rs_start(D)
     rs_step(C, 1)
-    rs_end(A)
+    gg_start(0)
     rs_end(B)
     rs_step(D, 1)
-    gg_start(A)
     rs_end(C)
-    gg_start(B)
+    z_send(1)
+    gg_step(0, 1)
     rs_end(D)
-    gg_step(A, 1)
-    gg_start(C)
-    gg_step(B, 1)
-    gg_start(D)
-    gg_step(A, 2)
-    gg_step(C, 1)
-    gg_end(B)
-    gg_step(D, 1)
-    gg_step(A, 3)
-    settle(2)
-    gg_end(C)
-    settle(3)
-    gg_end(D)
-    gg_end(A)
+    z_send(2)
+    gg_start(1)
+    gg_step(0, 2)
+    gg_start(2)
+    gg_step(0, 3)
+    gg_step(1, 1)
+    gg_end(0)
+    gg_step(2, 1)
+    gg_end(1)
+    zf_wait(1, 0, 0, 1, NY - 1, 2, NY - 2)
+    gg_end(2)
+    zf_wait(1, 1, 3, NY - 3, 4)
     settle(4)
-    settle(0)
-    settle(1)
-    for b in range(3):
-        mirror_wait(b)
-        settle(BLOCKS + b)
+    zf_wait(0, 0, *range(NY))
+    for b in range(4):
+        settle(b)
+    mirror_wait(2)
+    settle(7)
+    mirror_wait(0)
+    mirror_wait(1)
+    settle(5)
+    settle(6)
 
     def inner(ch):
         v = cubic_term * f32(mine(xg, ch)[...]) + quintic_term * dot(gl[...], xg[:, lanes(ch)])
@@ -426,8 +454,8 @@
     gw[1].near()
     gw[0].beyond()
     inner(3)
+    outer(0)
     gw[2].near()
-    outer(0)
     gw[1].beyond()
     gw[3].near()
     outer(1)
@@ -469,8 +497,9 @@
             dma((4,)), dma((4,)),
             dma((2, 4)), dma((2, 4, 6)),
             dma((n,)), dma((n, 4)),
-            dma((n,)), dma((n,)),
-            dma((n,)), dma((n, 4)),
+            dma((3,)), dma((3,)),
+            dma((3,)), dma((3, 4)),
+            dma((2,)), dma((2, 2)),
             dma((3,)), dma((3,)),
             dma((4,)), dma((4,)),
         ],

time: 110 us -> 109 us (level)
    pallas_call x1, Pallas kernels: 108 us -> 107 us  [on_device(): pl.pallas_call(kernel, out_shape=jax.ShapeDtypeStruct((PAD, local), bf),...]
where the time goes in v4:
time: 109 us
  Pallas kernels  107 us (98%)
  local copies, waits for them, and re-layouts  1.22 us (1%)
  other arithmetic  1.11 us (1%)
    pallas_call x1, Pallas kernels, on_device(): pl.pallas_call(kernel, out_shape=jax.ShapeDtypeStruct((PAD, local), bf),...  107 us

profile of v4, /device:TPU:1, one launch (start us, length us, event | category | flops | bytes accessed | tf_op | source)
XLA Modules:
  0.0 108.9 jit_solution(8856011376865765583)
XLA Ops:
  0.0 0.0 copy-start
  0.0 1.2 %copy-done = f32[42,5376]{1,0:T(8,128)S(1)} copy-done((f32[42,5376]{1,0:T(8,128)S(1)}, f32[42,5376]{1,0:T(8,128)}, u32[]{:S(2)}) %copy-start) | copy-done | bytes 903192
  1.2 106.5 %newton_schulz.1 = bf16[48,5376]{1,0:T(8,128)(2,1)S(1)} custom-call(f32[42,5376]{1,0:T(8,128)S(1)} %copy-done), custom_call_target="tpu_custom_call" | custom-call | tf_op jit(solution)/shard_map/newton_schulz/pallas_call | solution.py:476
  107.8 1.1 %add_multiply_fusion = f32[42,5376]{1,0:T(8,128)} fusion(bf16[48,5376]{1,0:T(8,128)(2,1)S(1)} %newton_schulz.1, f32[42,5376]{1,0:T(8,128)S(1)} %copy-done), kind=kLoop, calls=%fused_computation | loop fusion | flops 1354752 | bytes 2257920 | tf_op jit(solution)/shard_map/mul | solution.py:511
Async XLA Ops:
  0.0 1.2 %copy-start = (f32[42,5376]{1,0:T(8,128)S(1)}, f32[42,5376]{1,0:T(8,128)}, u32[]{:S(2)}) copy-start(f32[42,5376]{1,0:T(8,128)} %x_ref.1) | copy-start | bytes 2709508

commit v5 on v4

--- a/solution.py
+++ b/solution.py
@@ -32,7 +32,7 @@
     (1152, 384, 0, 3, True),
     (1536, 384, 1, 4, True),
 )
-GROUPS = ((0, 0, False, True), (768, 1, True, True), (1536, 1, True, False))
+GROUPS = ((0, 0, False, True), (768, 1, True, False), (1536, 1, True, False), (1152, 0, True, False))
 
 
 def dot(a, b, dims=((1,), (0,))):
@@ -181,17 +181,13 @@
             self.push(0, mine, self.ref(DOWN), east)
             self.push(1, mine, self.ref(UP), west)
             self.push(3, mine, mine, sibling)
-            if self.ch == 3:
-                self.push(2, mine, self.ref(self.far(x + 2)), dev(y, x + 2, c))
 
         def near(self):
             self.wait(0, self.ref(DOWN))
-            if self.ch < 3:
-                self.push(2, self.ref(DOWN, 0), self.ref(self.far(x + 1), 0), east)
+            self.push(2, self.ref(DOWN, 0), self.ref(self.far(x + 1), 0), east)
             self.push(4, self.ref(DOWN), self.ref(DOWN_PAIR), sibling)
             self.wait(1, self.ref(UP))
-            if self.ch < 3:
-                self.push(2, self.ref(UP, 1), self.ref(self.far(x + 3), 1), west)
+            self.push(2, self.ref(UP, 1), self.ref(self.far(x + 3), 1), west)
             self.push(4, self.ref(UP), self.ref(UP_PAIR), sibling)
 
         def beyond(self):
@@ -285,11 +281,9 @@
 
     def mirror(g, j, side):
         ref = gf.at[block(y + j), gat(g, side)]
-        if g == 1:
-            i = (side - z) % 2
-            send(ref, mx.at[side, block(y + j), :], mx_s.at[i], mx_r.at[i], dev(y, x + 1 + 2 * side, (c + side) % 2))
-        elif g == 2:
-            send(ref, mx.at[2, block(y + j), :], mx_s.at[2], mx_r.at[2], partners[2])
+        if g > 0:
+            b = (0, 2, 1)[g - 1]
+            send(ref, mx.at[b, block(y + j), :], mx_s.at[b], mx_r.at[b], partners[b])
 
     def spread_on(g, k, *js):
         for j in js:
@@ -322,11 +316,8 @@
         spread_on(g, 0, 0)
         if GROUPS[g][3]:
             leave(gf.at[:, 0:SLOT], zf_s.at[g])
-        if g == 1:
-            leave(gf.at[:, 0:SLOT], mx_s.at[0])
-            leave(gf.at[:, 0:SLOT], mx_s.at[1])
-        elif g == 2:
-            leave(gf.at[:, 0:SLOT], mx_s.at[2])
+        if g > 0:
+            leave(gf.at[:, 0:SLOT], mx_s.at[(0, 2, 1)[g - 1]])
 
     def gg_step(g, k):
         far = GROUPS[g][1]
@@ -397,33 +388,37 @@
     rs_step(C, 1)
     gg_start(0)
     rs_end(B)
+    z_send(1)
     rs_step(D, 1)
     rs_end(C)
-    z_send(1)
+    z_send(3)
     gg_step(0, 1)
+    gg_start(1)
     rs_end(D)
     z_send(2)
-    gg_start(1)
+    gg_start(3)
     gg_step(0, 2)
+    gg_step(1, 1)
     gg_start(2)
+    gg_step(3, 1)
     gg_step(0, 3)
-    gg_step(1, 1)
+    gg_end(1)
+    gg_step(2, 1)
+    gg_end(3)
     gg_end(0)
-    gg_step(2, 1)
-    gg_end(1)
-    zf_wait(1, 0, 0, 1, NY - 1, 2, NY - 2)
+    settle(2)
+    settle(3)
     gg_end(2)
-    zf_wait(1, 1, 3, NY - 3, 4)
+    zf_wait(0, 0, *range(NY))
+    settle(0)
+    settle(1)
     settle(4)
-    zf_wait(0, 0, *range(NY))
-    for b in range(4):
-        settle(b)
+    mirror_wait(0)
+    settle(5)
+    mirror_wait(1)
+    settle(6)
     mirror_wait(2)
     settle(7)
-    mirror_wait(0)
-    mirror_wait(1)
-    settle(5)
-    settle(6)
 
     def inner(ch):
         v = cubic_term * f32(mine(xg, ch)[...]) + quintic_term * dot(gl[...], xg[:, lanes(ch)])
@@ -454,8 +449,8 @@
     gw[1].near()
     gw[0].beyond()
     inner(3)
+    gw[2].near()
     outer(0)
-    gw[2].near()
     gw[1].beyond()
     gw[3].near()
     outer(1)
@@ -497,8 +492,8 @@
             dma((4,)), dma((4,)),
             dma((2, 4)), dma((2, 4, 6)),
             dma((n,)), dma((n, 4)),
-            dma((3,)), dma((3,)),
-            dma((3,)), dma((3, 4)),
+            dma((4,)), dma((4,)),
+            dma((4,)), dma((4, 4)),
             dma((2,)), dma((2, 2)),
             dma((3,)), dma((3,)),
             dma((4,)), dma((4,)),

time: 109 us -> 106 us (0.972)
  Pallas kernels: 107 us -> 103 us
    pallas_call x1, Pallas kernels: 107 us -> 103 us  [on_device(): pl.pallas_call(kernel, out_shape=jax.ShapeDtypeStruct((PAD, local), bf),...]
where the time goes in v5:
time: 106 us
  Pallas kernels  103 us (97%)
  local copies, waits for them, and re-layouts  1.22 us (1%)
  other arithmetic  1.11 us (1%)
    pallas_call x1, Pallas kernels, on_device(): pl.pallas_call(kernel, out_shape=jax.ShapeDtypeStruct((PAD, local), bf),...  103 us

profile of v5, /device:TPU:1, one launch (start us, length us, event | category | flops | bytes accessed | tf_op | source)
XLA Modules:
  0.0 105.6 jit_solution(3226447305028810191)
XLA Ops:
  0.0 0.0 copy-start
  0.0 1.2 %copy-done = f32[42,5376]{1,0:T(8,128)S(1)} copy-done((f32[42,5376]{1,0:T(8,128)S(1)}, f32[42,5376]{1,0:T(8,128)}, u32[]{:S(2)}) %copy-start) | copy-done | bytes 903192
  1.2 103.2 %newton_schulz.1 = bf16[48,5376]{1,0:T(8,128)(2,1)S(1)} custom-call(f32[42,5376]{1,0:T(8,128)S(1)} %copy-done), custom_call_target="tpu_custom_call" | custom-call | tf_op jit(solution)/shard_map/newton_schulz/pallas_call | solution.py:471
  104.5 1.1 %add_multiply_fusion = f32[42,5376]{1,0:T(8,128)} fusion(bf16[48,5376]{1,0:T(8,128)(2,1)S(1)} %newton_schulz.1, f32[42,5376]{1,0:T(8,128)S(1)} %copy-done), kind=kLoop, calls=%fused_computation | loop fusion | flops 1354752 | bytes 2257920 | tf_op jit(solution)/shard_map/mul | solution.py:506
Async XLA Ops:
  0.0 1.2 %copy-start = (f32[42,5376]{1,0:T(8,128)S(1)}, f32[42,5376]{1,0:T(8,128)}, u32[]{:S(2)}) copy-start(f32[42,5376]{1,0:T(8,128)} %x_ref.1) | copy-start | bytes 2709508

commit v6 on v5

--- a/solution.py
+++ b/solution.py
@@ -21,7 +21,7 @@
 DENSE = NY * OWN
 SLOT = NY * PAD
 WIDE = 768
-CUTS = ((0, 128), (128, 256), (384, 256), (640, 128))
+CUTS = ((0, 256), (256, 256), (512, 128), (640, 128))
 ORDER = (4, 3, 5, 2, 6, 1, 7)
 UP, DOWN_PAIR, FAR, DOWN, UP_PAIR = 2, 3, 4, 5, 6
 BLOCKS = 5
@@ -362,11 +362,11 @@
     share(2)
     gx[0].near()
     share(3)
-    gx[1].near()
     pairs(3)
     gram(0)
     gram(1)
     rs_start(A)
+    gx[1].near()
     gx[2].near()
     gx[0].beyond()
     gx[3].near()

time: 106 us -> 105 us (level)
  no operation moved by 1% of the time
where the time goes in v6:
time: 105 us
  Pallas kernels  102 us (97%)
  local copies, waits for them, and re-layouts  1.22 us (1%)
  other arithmetic  1.11 us (1%)
    pallas_call x1, Pallas kernels, on_device(): pl.pallas_call(kernel, out_shape=jax.ShapeDtypeStruct((PAD, local), bf),...  102 us

profile of v6, /device:TPU:1, one launch (start us, length us, event | category | flops | bytes accessed | tf_op | source)
XLA Modules:
  0.0 104.7 jit_solution(5408445582010694999)
XLA Ops:
  0.0 0.0 copy-start
  0.0 1.2 %copy-done = f32[42,5376]{1,0:T(8,128)S(1)} copy-done((f32[42,5376]{1,0:T(8,128)S(1)}, f32[42,5376]{1,0:T(8,128)}, u32[]{:S(2)}) %copy-start) | copy-done | bytes 903192
  1.2 102.4 %newton_schulz.1 = bf16[48,5376]{1,0:T(8,128)(2,1)S(1)} custom-call(f32[42,5376]{1,0:T(8,128)S(1)} %copy-done), custom_call_target="tpu_custom_call" | custom-call | tf_op jit(solution)/shard_map/newton_schulz/pallas_call | solution.py:471
  103.6 1.1 %add_multiply_fusion = f32[42,5376]{1,0:T(8,128)} fusion(bf16[48,5376]{1,0:T(8,128)(2,1)S(1)} %newton_schulz.1, f32[42,5376]{1,0:T(8,128)S(1)} %copy-done), kind=kLoop, calls=%fused_computation | loop fusion | flops 1354752 | bytes 2257920 | tf_op jit(solution)/shard_map/mul | solution.py:506
Async XLA Ops:
  0.0 1.2 %copy-start = (f32[42,5376]{1,0:T(8,128)S(1)}, f32[42,5376]{1,0:T(8,128)}, u32[]{:S(2)}) copy-start(f32[42,5376]{1,0:T(8,128)} %x_ref.1) | copy-start | bytes 2709508

commit v7 on v6

--- a/solution.py
+++ b/solution.py
@@ -170,11 +170,15 @@
             return FAR + 3 * ((xx % NX) // 2)
 
         def push(self, q, src, dst, to):
-            rsem = ag_r.at[self.n, 0 if q > 2 and self.n == 0 else self.ch, q]
-            send(src, dst, ag_s.at[self.n, self.ch], rsem, to)
+            send(src, dst, ag_s.at[self.n, self.ch], ag_r.at[self.sem(q)], to)
+
+        def sem(self, q):
+            if self.n == 0:
+                return self.ch * 3 + q if q < 3 else 9 + q
+            return 15 + self.ch * 4 + min(q, 3)
 
         def wait(self, q, ref):
-            arrive(ref, ag_r.at[self.n, self.ch, q])
+            arrive(ref, ag_r.at[self.sem(q)])
 
         def start(self):
             mine = self.ref(c)
@@ -196,14 +200,13 @@
             leave(self.buf.at[0:7 * DENSE, lanes(self.ch)], ag_s.at[self.n, self.ch])
 
         def pairs(self):
-            for q, rows in ((3, 1), (4, 2), (5, 1)):
-                self.wait(q, self.buf.at[0:rows * DENSE, lanes(self.ch)])
+            self.wait(3, self.buf.at[0:4 * DENSE, lanes(self.ch)])
 
     gx = [Gather(xg, 0, ch) for ch in range(4)]
     gw = [Gather(wg, 1, ch) for ch in range(4)]
 
     def pairs(q):
-        arrive(xg.at[0:(2 if q == 4 else 1) * DENSE, :], ag_r.at[0, 0, q])
+        arrive(xg.at[0:(2 if q == 4 else 1) * DENSE, :], ag_r.at[9 + q])
 
     def mine(buf, ch):
         return buf.at[pl.ds(pl.multiple_of(c * SLOT, 16), SLOT), lanes(ch)]
@@ -299,10 +302,10 @@
 
     def gg_send(g, j, k, to):
         ref = gf.at[block(y + j), gat(g, z)]
-        send(ref, ref, gg_s.at[g], gg_r.at[g, k], to)
+        send(ref, ref, gg_s.at[g], gg_r.at[k if g == 0 else 2 * g + 2 + k], to)
 
     def gg_wait(g, k, n):
-        arrive(gf.at[0:n * PAD, 0:SLOT], gg_r.at[g, k])
+        arrive(gf.at[0:n * PAD, 0:SLOT], gg_r.at[k if g == 0 else 2 * g + 2 + k])
 
     def gg_start(g):
         here = gat(g, z)
@@ -490,11 +493,11 @@
             pltpu.VMEM((SLOT, NP * SLOT), bf),
             pltpu.VMEM((SLOT, WIDE), bf),
             dma((4,)), dma((4,)),
-            dma((2, 4)), dma((2, 4, 6)),
-            dma((n,)), dma((n, 4)),
+            dma((2, 4)), dma((31,)),
+            dma((n,)), dma((n, 2)),
             dma((4,)), dma((4,)),
-            dma((4,)), dma((4, 4)),
-            dma((2,)), dma((2, 2)),
+            dma((4,)), dma((10,)),
+            dma((1,)), dma((1, 1)),
             dma((3,)), dma((3,)),
             dma((4,)), dma((4,)),
         ],

time: 105 us -> 105 us (level)
  no operation moved by 1% of the time
where the time goes in v7:
time: 105 us; the launch traced here: 104 us
  Pallas kernels  102 us (97%)
  local copies, waits for them, and re-layouts  1.22 us (1%)
  other arithmetic  1.11 us (1%)
    pallas_call x1, Pallas kernels, on_device(): pl.pallas_call(kernel, out_shape=jax.ShapeDtypeStruct((PAD, local), bf),...  102 us

profile of v7, /device:TPU:1, one launch (start us, length us, event | category | flops | bytes accessed | tf_op | source)
XLA Modules:
  0.0 104.4 jit_solution(5292601869583285842)
XLA Ops:
  0.0 0.0 copy-start
  0.0 1.2 %copy-done = f32[42,5376]{1,0:T(8,128)S(1)} copy-done((f32[42,5376]{1,0:T(8,128)S(1)}, f32[42,5376]{1,0:T(8,128)}, u32[]{:S(2)}) %copy-start) | copy-done | bytes 903192
  1.2 102.0 %newton_schulz.1 = bf16[48,5376]{1,0:T(8,128)(2,1)S(1)} custom-call(f32[42,5376]{1,0:T(8,128)S(1)} %copy-done), custom_call_target="tpu_custom_call" | custom-call | tf_op jit(solution)/shard_map/newton_schulz/pallas_call | solution.py:474
  103.3 1.1 %add_multiply_fusion = f32[42,5376]{1,0:T(8,128)} fusion(bf16[48,5376]{1,0:T(8,128)(2,1)S(1)} %newton_schulz.1, f32[42,5376]{1,0:T(8,128)S(1)} %copy-done), kind=kLoop, calls=%fused_computation | loop fusion | flops 1354752 | bytes 2257920 | tf_op jit(solution)/shard_map/mul | solution.py:509
Async XLA Ops:
  0.0 1.2 %copy-start = (f32[42,5376]{1,0:T(8,128)S(1)}, f32[42,5376]{1,0:T(8,128)}, u32[]{:S(2)}) copy-start(f32[42,5376]{1,0:T(8,128)} %x_ref.1) | copy-start | bytes 2709508
